TPU v7x, 512 devices: a whole 4x8x8 slice. The times are simulated.
512 devices in a mesh: grp: 32 (over y, x), slab: 16 (over z, core).
Axes of the slice: x: 4, y: 8, z: 8, core: 2. Of those that a mesh axis runs over, the one named last changes fastest.
Arguments:
- hall_now: float32 [32, 256, 128, 128], P('grp', None, 'slab'), may hold values from -6 to 6
- hall_prev: float32 [32, 256, 128, 128], P('grp', None, 'slab'), may hold values from -6 to 6
- room_now: float32 [32, 16, 32, 32, 128], P('grp', 'slab'), may hold values from -6 to 6
- room_prev: float32 [32, 16, 32, 32, 128], P('grp', 'slab'), may hold values from -6 to 6
- room_length: int32 [32, 16, 32], P('grp', 'slab'), may hold values from 16 to 32
- right_neighbor: int32 [16, 1024], P('slab'), may hold values from 0 to 1023, as said below
Outputs:
- hall_pressure: float32 [32, 256, 128, 128], P('grp', 'slab')
- room_pressure: float32 [32, 16, 32, 32, 128], P('grp', 'slab')
Inputs may be any that keep to these rules, and one draw needn't show every extreme that they name: For each index of slab, right_neighbor is a permutation of the 1024 room partitions, numbered grp index times 32 plus slot. Slot p of grp index g has its right neighbour at grp index (g + s) mod 32, where s depends only on the index of slab and on p. At most 2 of one device's partitions have their right neighbour on any one device, and exactly 2 do for some device.
All inputs are finite; a program needn't handle non-finite values.
Results may differ from a plain program's by a relative error of at most 0.0003.
Values sent between devices are 32-bit elements; how exact they have to be, the bound alone decides.
A program may use at most 64 MiB of HBM per device.

v0:
```python
import functools
import math

import jax
import jax.numpy as jnp
import ml_dtypes
import numpy as np
from jax import lax
from jax.experimental import pallas as pl
from jax.experimental.pallas import tpu as pltpu
from jax.sharding import PartitionSpec as P

SY = 8
SZ = 16
STEPS = 4
SHORTEST = 16
TIME_STEP = 0.4
SCALE = (TIME_STEP * math.pi) ** 2
STENCIL = np.array([[270, -27, 2], [-27, 2, 0], [2, 0, 0]], np.float64) / 180.0
F32 = jnp.float32
BF16 = jnp.bfloat16
MESH = pl.DeviceIdType.MESH


def dct(length):
    k = np.arange(length)[:, None]
    i = np.arange(length)[None, :]
    w = np.where(k == 0, np.sqrt(1.0 / length), np.sqrt(2.0 / length))
    return w * np.cos(np.pi * k * (2 * i + 1) / (2 * length))


def halves(x):
    high = x.astype(np.float32).astype(ml_dtypes.bfloat16)
    low = (x - high.astype(np.float64)).astype(ml_dtypes.bfloat16)
    return high, low


def left_table(x):
    high, low = halves(x)
    return np.concatenate([high, high, low], axis=1)


def right_table(x):
    high, low = halves(x)
    return np.concatenate([high, high, low], axis=0)


def face_rows(table):
    length = table.shape[0]
    sign = np.where(np.arange(length) % 2 == 0, 1.0, -1.0)
    low = table[:, :3].T
    forced = STENCIL.T @ low
    zero = np.zeros((2, length))
    return (
        np.concatenate([low, low * sign, zero], axis=0),
        np.concatenate([forced, forced * sign, zero], axis=0),
    )


def hall_tables(nx, ny, nz):
    faces, forced = face_rows(dct(nz))
    high, low = halves(faces)
    spread = np.concatenate(
        [np.concatenate([high, high], axis=1), np.concatenate([low, 0 * low], axis=1)], axis=0
    )
    pairs = np.concatenate([forced[k : k + 1] * faces for k in range(6)], axis=0)
    high, low = halves(pairs)
    respond = np.concatenate(
        [np.concatenate([high, high], axis=1), np.concatenate([low, 0 * low], axis=1)], axis=0
    )
    high, low = halves(forced)
    outer = np.concatenate([high, high, low, low], axis=0)
    return spread, respond, outer, left_table(dct(nx).T), left_table(dct(ny).T), right_table(dct(nz))


def room_tables(width):
    faces, forced, full = [], [], []
    for length in range(SHORTEST, width + 1):
        table = np.zeros((width, width))
        table[:length, :length] = dct(length)
        low, high = face_rows(table[:, :])
        faces.append(np.tile(low, (1, 4)))
        forced.append(np.tile(high, (1, 4)))
        full.append(np.tile(table.T, (1, 4)))
    return [np.stack(t).astype(np.float32) for t in (faces, forced, full)]


def factors(q):
    h = jnp.full_like(q, 2.0 / math.factorial(18))
    for n in range(7, -1, -1):
        h = 2.0 / math.factorial(2 * n + 2) - h * q
    return 2.0 - q * h, (TIME_STEP * TIME_STEP) * h


def mm(a, b):
    return jnp.dot(a, b, preferred_element_type=F32)


def mm_nt(a, b):
    return lax.dot_general(a, b, (((1,), (1,)), ((), ())), preferred_element_type=F32)


def split(x):
    high = x.astype(BF16)
    return high, (x - high.astype(F32)).astype(BF16)


def stacked(x, axis):
    high, low = split(x)
    return jnp.concatenate([high, low, high], axis=axis)


def iota(shape, dim):
    return lax.broadcasted_iota(jnp.int32, shape, dim).astype(F32)


def total(mask, values, axis):
    return jnp.sum(jnp.where(mask, values, 0.0), axis=axis, keepdims=True)


def kernel(
    groups, slabs, count,
    hall_now, hall_prev, room_now, room_prev, lengths, ids, shifts,
    spread_t, respond_t, outer_t, cosx_t, cosy_t, cosz_t, face_t, force_t, room_t, cross_t,
    hall_out, room_out,
    hall_c2, hall_gain, hall_base, hall_faces, hall_resp, hall_diff, hall_other,
    hall_send, hall_recv, a2a_send, a2a_recv,
    room_c2, room_gain, room_a, room_b, room_faces, raw_faces, raw_force, raw_full,
    face_l, force_l, full_l, pack_l, take_l, room_send, room_recv,
    hall_ssem, hall_rsem, a2a_ssem, a2a_rsem, room_ssem, room_rsem,
):
    me = lax.axis_index("grp")
    column = lax.axis_index("slab")
    nx, part_y, nz = hall_now.shape
    ny = part_y * slabs
    part_x = nx // slabs
    lanes = nx * part_y
    width = room_now.shape[0] // count
    batches = count // 4

    barrier = pltpu.get_barrier_semaphore()

    def greet_grp(step, carry):
        pl.semaphore_signal(
            barrier, inc=1, device_id=(lax.rem(me + step, groups), column), device_id_type=MESH
        )
        return carry

    def greet_slab(step, carry):
        pl.semaphore_signal(
            barrier, inc=1, device_id=(me, lax.rem(column + step, slabs)), device_id_type=MESH
        )
        return carry

    lax.fori_loop(1, groups, greet_grp, 0)
    lax.fori_loop(1, slabs, greet_slab, 0)

    chunk = 256
    deep = chunk // part_y

    def spread_of(x):
        high, low = split(x)
        both = mm_nt(spread_t[...], jnp.concatenate([high, low], axis=1))
        return both[:8] + both[8:]

    def first_faces(i, carry):
        x = hall_now[pl.ds(i * deep, deep)].reshape(chunk, nz)
        hall_faces[0, :, pl.ds(pl.multiple_of(i * chunk, chunk), chunk)] = spread_of(x)
        return carry

    lax.fori_loop(0, lanes // chunk, first_faces, 0)

    def hall_copy(t, side):
        peer = lax.rem(me + (1 if side == 0 else groups - 1), groups)
        return pltpu.make_async_remote_copy(
            src_ref=hall_send.at[t, side],
            dst_ref=hall_recv.at[t, side],
            send_sem=hall_ssem.at[t, side],
            recv_sem=hall_rsem.at[t, side],
            device_id=(peer, column),
            device_id_type=MESH,
        )

    def hall_put(t):
        own = hall_faces[t]
        for k in range(3):
            for j in range(lanes // 128):
                cut = slice(128 * j, 128 * j + 128)
                hall_send[t, 0, k, j : j + 1, :] = own[3 + k : 4 + k, cut]
                hall_send[t, 1, k, j : j + 1, :] = own[k : k + 1, cut]
        hall_copy(t, 0).start()
        hall_copy(t, 1).start()

    def hall_get(t):
        hall_copy(t, 0).wait_recv()
        hall_copy(t, 1).wait_recv()
        for k in range(3):
            for j in range(lanes // 128):
                cut = slice(128 * j, 128 * j + 128)
                hall_other[k : k + 1, cut] = hall_recv[t, 0, k, j : j + 1, :]
                hall_other[3 + k : 4 + k, cut] = hall_recv[t, 1, k, j : j + 1, :]
        row = lax.broadcasted_iota(jnp.int32, (8, lanes), 0)
        first = jnp.where(me > 0, 0, 3)
        last = jnp.where(me < groups - 1, 6, 3)
        diff = jnp.where((row >= first) & (row < last), hall_other[...] - hall_faces[t], 0.0)
        hall_diff[t] = diff
        return diff

    def hall_respond(t, lag, diff):
        acc = hall_faces[t + lag]
        for k in range(6):
            acc = acc + hall_resp[lag - 1, 8 * k : 8 * k + 8, :] * diff[k : k + 1, :]
        hall_faces[t + lag] = acc

    def hall_accumulate(t):
        def body(i, carry):
            at = pl.ds(i * deep, deep)
            e = hall_diff[t, :, pl.ds(pl.multiple_of(i * chunk, chunk), chunk)]
            high = e.astype(BF16).astype(F32)
            low = e - high
            e = jnp.concatenate([high, low, high, low], axis=0).T.astype(BF16)
            forced = mm(e, outer_t[...]).reshape(deep, part_y, nz)
            c2 = hall_c2[at]
            weight = hall_gain[at]
            if t == 2:
                weight = weight * c2
            elif t == 1:
                weight = weight * (c2 * c2 - 1.0)
            elif t == 0:
                weight = weight * (c2 * (c2 * c2 - 2.0))
            hall_base[at] = hall_base[at] + weight * forced
            return carry

        lax.fori_loop(0, lanes // chunk, body, 0)

    hall_other[...] = jnp.zeros_like(hall_other)
    pl.semaphore_wait(barrier, groups + slabs - 2)
    hall_put(0)

    lane = lax.broadcasted_iota(jnp.int32, (width, 128), 1)
    kx = lax.broadcasted_iota(jnp.int32, (width, 128), 0)
    q_cross = (lane // SZ).astype(F32) / SY
    q_cross = SCALE * (q_cross * q_cross)
    z_part = (lane % SZ).astype(F32) / SZ
    q_cross = q_cross + SCALE * (z_part * z_part)
    kx_f = kx.astype(F32)
    kx_sq = SCALE * (kx_f * kx_f)

    def room_setup(b, carry):
        for i in range(4):
            r = 4 * b + i
            length = lengths[r]
            which = jnp.maximum(length - SHORTEST, 0)
            at = pl.ds(pl.multiple_of(r * width, width), width)
            at8 = pl.ds(pl.multiple_of(r * 8, 8), 8)
            mine = lane // width == i
            raw_faces[at8, :] = jnp.where(mine[:8], face_t[which], 0.0)
            raw_force[at8, :] = jnp.where(mine[:8], force_t[which], 0.0)
            raw_full[at, :] = jnp.where(mine, room_t[which], 0.0)
            extent = jnp.full((width, 128), length, jnp.int32)
            live = kx < extent
            extent = extent.astype(F32)
            c2, gain = factors(kx_sq / (extent * extent) + q_cross)
            room_c2[at, :] = c2
            room_gain[at, :] = gain
            room_a[at, :] = jnp.where(live, room_now[at, :], 0.0)
            room_b[at, :] = jnp.where(live, room_prev[at, :], 0.0)
        return carry

    lax.fori_loop(0, batches, room_setup, 0)

    for b in range(batches):
        cut = slice(32 * b, 32 * b + 32)
        high, low = split(raw_faces[cut, :])
        face_l[cut, :] = jnp.concatenate([high, high, low], axis=1)
        x = raw_force[cut, :]
        high = x.astype(BF16).astype(F32)
        low = x - high
        big = slice(128 * b, 128 * b + 128)
        force_l[big, :] = jnp.concatenate([high, high, low, low], axis=0).T.astype(BF16)
        high, low = split(raw_full[big, :])
        full_l[big, :] = jnp.concatenate([high, high, low], axis=1)
        room_faces[cut, :] = mm(face_l[cut, :], stacked(room_a[big, :], 0))

    bits = int(math.log2(count))
    wide = 8 * count
    s_col = (ids[:, 0:1] >> bits).astype(F32)
    s_row = shifts[...].astype(F32)
    p_col = iota((count, wide), 0)
    lane_i = lax.broadcasted_iota(jnp.int32, (count, wide), 1)
    p_row = (lane_i >> 3).astype(F32)
    f_row = (lane_i & 7).astype(F32)
    same = s_col == s_row
    rank_row = total(same & (p_col < p_row), 1.0, 0)
    rank_col = total(same & (p_row < p_col) & (f_row == 0.0), 1.0, 1)
    home = me.astype(F32) - s_col
    home = jnp.where(home < 0.0, home + groups, home)
    landing = total(iota((count, groups), 1) == home, (ids[...] & (count - 1)).astype(F32), 1)
    match = landing == p_row
    ls_row = total(match, jnp.broadcast_to(s_col, (count, wide)), 0)
    lr_row = total(match, jnp.broadcast_to(rank_col, (count, wide)), 0)

    def back(s):
        return jnp.where(s == 0.0, 0.0, groups - s)

    f = f_row[0:1]
    layer = jnp.where(f < 3.0, f, f - 3.0)
    pack_row = jnp.where(
        f < 3.0, 16.0 * back(ls_row) + 6.0 + 3.0 * lr_row + layer, 16.0 * s_row + 3.0 * rank_row + layer
    )
    take_row = jnp.where(
        f < 3.0, 16.0 * ls_row + 3.0 * lr_row + layer, 16.0 * back(s_row) + 6.0 + 3.0 * rank_row + layer
    )
    pack_row = jnp.where(f < 6.0, pack_row, -1.0)
    take_row = jnp.where(f < 6.0, take_row, -1.0)
    slots = 16 * groups
    hot = jnp.where(iota((slots, wide), 0) == pack_row, 1.0, 0.0).astype(BF16)
    pack_l[...] = jnp.concatenate([hot, hot], axis=1)
    take_col = jnp.broadcast_to(take_row, (8, wide)).T[:, 0:1]
    hot = jnp.where(iota((wide, slots), 1) == take_col, 1.0, 0.0).astype(BF16)
    take_l[...] = jnp.concatenate([hot, hot], axis=1)

    def room_copy(t, step):
        return pltpu.make_async_remote_copy(
            src_ref=room_send.at[t, step],
            dst_ref=room_recv.at[t, step - 1],
            send_sem=room_ssem.at[t, step - 1],
            recv_sem=room_rsem.at[t, step - 1],
            device_id=(lax.rem(me + step, groups), column),
            device_id_type=MESH,
        )

    def room_put(t):
        high, low = split(room_faces[...])
        packed = mm(pack_l[...], jnp.concatenate([high, low], axis=0))
        room_send[t] = packed.reshape(groups, 16, 128)[:, :12, :]

        def body(step, carry):
            room_copy(t, step).start()
            return carry

        lax.fori_loop(1, groups, body, 0)

    def room_get(t):
        def body(step, carry):
            room_copy(t, step).wait_recv()
            return carry

        lax.fori_loop(1, groups, body, 0)
        got = jnp.concatenate([room_send[t, 0:1], room_recv[t]], axis=0)
        got = jnp.concatenate([got, jnp.zeros((groups, 4, 128), F32)], axis=1).reshape(slots, 128)
        high, low = split(got)
        other = mm(take_l[...], jnp.concatenate([high, low], axis=0))
        return other - room_faces[...]

    def room_step(t):
        diff = room_get(t)
        now, prev = (room_a, room_b) if t % 2 == 0 else (room_b, room_a)
        for b in range(batches):
            cut = slice(32 * b, 32 * b + 32)
            big = slice(128 * b, 128 * b + 128)
            high, low = split(diff[cut])
            forced = mm(force_l[big, :], jnp.concatenate([high, low, high, low], axis=0))
            fresh = room_c2[big, :] * now[big, :] - prev[big, :] + room_gain[big, :] * forced
            if t < STEPS - 1:
                prev[big, :] = fresh
                room_faces[cut, :] = mm(face_l[cut, :], stacked(fresh, 0))
            else:
                x = mm(full_l[big, :], stacked(fresh, 0))
                room_out[big, :] = mm(stacked(x, 1), cross_t[...])
        if t < STEPS - 1:
            room_put(t + 1)

    room_put(0)

    yz = lax.broadcasted_iota(jnp.int32, (part_y, nz), 0) + column * part_y
    ky_f = yz.astype(F32)
    kz_f = iota((part_y, nz), 1)
    q_yz = (SCALE / ny**2) * (ky_f * ky_f) + (SCALE / nz**2) * (kz_f * kz_f)

    def prepare(i, carry):
        at = pl.ds(i * deep, deep)
        cols = pl.ds(pl.multiple_of(i * chunk, chunk), chunk)
        a = (lax.broadcasted_iota(jnp.int32, (deep, part_y, nz), 0) + i * deep).astype(F32)
        c2, gain = factors((SCALE / nx**2) * (a * a) + q_yz[None])
        hall_c2[at] = c2
        hall_gain[at] = gain
        now = hall_now[at]
        prev = hall_prev[at]
        s_now = gain
        s_prev = jnp.zeros_like(gain)
        for t in range(1, STEPS):
            now, prev = c2 * now - prev, now
            hall_faces[t, :, cols] = spread_of(now.reshape(chunk, nz))
            high, low = split(s_now.reshape(chunk, nz))
            both = mm_nt(respond_t[...], jnp.concatenate([high, low], axis=1))
            hall_resp[t - 1, :, cols] = both[:48] + both[48:]
            s_now, s_prev = c2 * s_now - s_prev, s_now
        hall_base[at] = c2 * now - prev
        return carry

    lax.fori_loop(0, lanes // chunk, prepare, 0)

    def hall_step(t):
        diff = hall_get(t)
        if t < STEPS - 1:
            hall_respond(t, 1, diff)
            hall_put(t + 1)
            for lag in range(2, STEPS - t):
                hall_respond(t, lag, diff)
        hall_accumulate(t)

    hall_step(0)
    hall_step(1)
    room_step(0)
    hall_step(2)
    hall_step(3)

    for b in range(part_y):
        a2a_send[b] = mm(cosx_t[...], stacked(hall_base[:, b, :], 0))

    def a2a_copy(step):
        peer = lax.rem(column + step, slabs)
        return pltpu.make_async_remote_copy(
            src_ref=a2a_send.at[:, pl.ds(pl.multiple_of(peer * part_x, part_x), part_x), :],
            dst_ref=a2a_recv.at[pl.ds(column * part_y, part_y)],
            send_sem=a2a_ssem.at[step],
            recv_sem=a2a_rsem.at[step],
            device_id=(me, peer),
            device_id_type=MESH,
        )

    def a2a_start(step, carry):
        a2a_copy(step).start()
        return carry

    lax.fori_loop(1, slabs, a2a_start, 0)

    def z_part_of(x):
        x = stacked(x.reshape(part_y * part_x, nz), 1)
        return mm(x, cosz_t[...]).reshape(part_y, part_x, nz)

    own = pl.ds(pl.multiple_of(column * part_x, part_x), part_x)
    a2a_recv[pl.ds(column * part_y, part_y)] = z_part_of(a2a_send[:, own, :])

    for t in range(1, STEPS):
        room_step(t)

    def a2a_take(step, carry):
        a2a_copy(step).wait_recv()
        source = lax.rem(column + slabs - step, slabs)
        at = pl.ds(source * part_y, part_y)
        a2a_recv[at] = z_part_of(a2a_recv[at])
        return carry

    lax.fori_loop(1, slabs, a2a_take, 0)
    for x in range(0, part_x, 2):
        pair = jnp.concatenate([stacked(a2a_recv[:, x, :], 0), stacked(a2a_recv[:, x + 1, :], 0)], axis=1)
        y = mm(cosy_t[...], pair)
        hall_out[x] = y[:, :nz]
        hall_out[x + 1] = y[:, nz:]

    for t in range(STEPS):
        hall_copy(t, 0).wait_send()
        hall_copy(t, 1).wait_send()

        def sent(step, carry):
            room_copy(t, step).wait_send()
            return carry

        lax.fori_loop(1, groups, sent, 0)

    def a2a_sent(step, carry):
        a2a_copy(step).wait_send()
        return carry

    lax.fori_loop(1, slabs, a2a_sent, 0)


def local(hall_now, hall_prev, room_now, room_prev, room_length, right_neighbor):
    groups = lax.axis_size("grp")
    slabs = lax.axis_size("slab")
    _, nx, part_y, nz = hall_now.shape
    _, _, count, width, cross = room_now.shape
    ny = part_y * slabs
    part_x = nx // slabs
    lanes = nx * part_y
    slots = 16 * groups
    ids = right_neighbor[0].reshape(groups, count)
    shifts = jnp.repeat(ids[0] // count, 8)[None, :]
    tables = [jnp.asarray(t) for t in hall_tables(nx, ny, nz)]
    tables += [jnp.asarray(t) for t in room_tables(width)]
    tables += [jnp.asarray(right_table(np.kron(dct(SY), dct(SZ))))]
    vmem = pl.BlockSpec(memory_space=pltpu.VMEM)
    smem = pl.BlockSpec(memory_space=pltpu.SMEM)
    rows = count * width
    dma = pltpu.SemaphoreType.DMA
    hall_pressure, room_pressure = pl.pallas_call(
        functools.partial(kernel, groups, slabs, count),
        out_shape=(
            jax.ShapeDtypeStruct((part_x, ny, nz), F32),
            jax.ShapeDtypeStruct((rows, cross), F32),
        ),
        in_specs=[vmem] * 4 + [smem] + [vmem] * (2 + len(tables)),
        out_specs=(vmem, vmem),
        scratch_shapes=[
            pltpu.VMEM((nx, part_y, nz), F32),
            pltpu.VMEM((nx, part_y, nz), F32),
            pltpu.VMEM((nx, part_y, nz), F32),
            pltpu.VMEM((STEPS, 8, lanes), F32),
            pltpu.VMEM((STEPS - 1, 48, lanes), F32),
            pltpu.VMEM((STEPS, 8, lanes), F32),
            pltpu.VMEM((8, lanes), F32),
            pltpu.VMEM((STEPS, 2, 3, lanes // 128, 128), F32),
            pltpu.VMEM((STEPS, 2, 3, lanes // 128, 128), F32),
            pltpu.VMEM((part_y, nx, nz), F32),
            pltpu.VMEM((ny, part_x, nz), F32),
            pltpu.VMEM((rows, cross), F32),
            pltpu.VMEM((rows, cross), F32),
            pltpu.VMEM((rows, cross), F32),
            pltpu.VMEM((rows, cross), F32),
            pltpu.VMEM((8 * count, cross), F32),
            pltpu.VMEM((8 * count, 4 * width), F32),
            pltpu.VMEM((8 * count, 4 * width), F32),
            pltpu.VMEM((rows, 4 * width), F32),
            pltpu.VMEM((8 * count, 12 * width), BF16),
            pltpu.VMEM((rows, 128), BF16),
            pltpu.VMEM((rows, 12 * width), BF16),
            pltpu.VMEM((slots, 16 * count), BF16),
            pltpu.VMEM((8 * count, 2 * slots), BF16),
            pltpu.VMEM((STEPS, groups, 12, 128), F32),
            pltpu.VMEM((STEPS, groups - 1, 12, 128), F32),
            dma((STEPS, 2)),
            dma((STEPS, 2)),
            dma((slabs,)),
            dma((slabs,)),
            dma((STEPS, groups - 1)),
            dma((STEPS, groups - 1)),
        ],
        compiler_params=pltpu.CompilerParams(
            collective_id=0, has_side_effects=True, vmem_limit_bytes=48 * 1024 * 1024
        ),
    )(
        hall_now[0],
        hall_prev[0],
        room_now.reshape(rows, cross),
        room_prev.reshape(rows, cross),
        room_length.reshape(count),
        ids.T,
        shifts,
        *tables,
    )
    return (hall_pressure[None], room_pressure.reshape(1, 1, count, width, cross))


def solution(mesh):
    in_specs = (
        P("grp", None, "slab", None),
        P("grp", None, "slab", None),
        P("grp", "slab", None, None, None),
        P("grp", "slab", None, None, None),
        P("grp", "slab", None),
        P("slab", None),
    )
    out_specs = (P("grp", "slab", None, None), P("grp", "slab", None, None, None))
    return jax.shard_map(local, mesh=mesh, in_specs=in_specs, out_specs=out_specs, check_vma=False)
```

profile of v0, /device:TPU:1, one launch (start us, length us, event | category | flops | bytes accessed | tf_op | source)
XLA Modules:
  0.0 92.6 jit_solution(3490921472624222251)
XLA Ops:
  0.6 0.0 copy-start.6
  0.6 0.7 and_select_fusion
  1.3 0.5 broadcast.12
  1.9 1.3 %reduce.3 = s32[1024]{0:T(1024)S(1)} reduce(s32[1,1024]{1,0:T(1,128)} %param.21, s32[]{:T(128)} %broadcast.12), dimensions={0}, to_apply=%param.21.reduce_sub_computation.3 | reduce | bytes 8196 | tf_op args[5]
  3.2 0.1 reshape_squeeze.3
  3.3 0.1 copy.18
  3.3 0.1 broadcast_in_dim.6
  3.4 0.0 copy-start.12
  3.4 0.0 copy-start.13
  3.4 0.0 copy-start.14
  3.4 0.1 broadcast_in_dim_reshape.3.shifts
  3.5 0.0 copy-done.6
  3.5 0.6 copy-done.12
  4.1 0.0 copy-done.13
  4.1 0.0 copy-done.14
  4.1 0.0 copy-start
  4.1 1.2 %copy-done = f32[1,256,8,128]{3,2,1,0:T(8,128)S(1)} copy-done((f32[1,256,8,128]{3,2,1,0:T(8,128)S(1)}, f32[1,256,8,128]{3,2,1,0:T(8,128)}, u32[]{:S(2)}) %copy-start) | copy-done | bytes 1048600
  5.4 0.0 copy-start.1
  5.4 1.2 %copy-done.1 = f32[1,256,8,128]{3,2,1,0:T(8,128)S(1)} copy-done((f32[1,256,8,128]{3,2,1,0:T(8,128)S(1)}, f32[1,256,8,128]{3,2,1,0:T(8,128)}, u32[]{:S(2)}) %copy-start.1) | copy-done | bytes 1048600
  6.6 0.0 copy-start.2
  6.6 1.0 %copy-done.2 = f32[1,1,32,32,128]{4,3,2,1,0:T(8,128)S(1)} copy-done((f32[1,1,32,32,128]{4,3,2,1,0:T(8,128)S(1)}, f32[1,1,32,32,128]{4,3,2,1,0:T(8,128)}, u32[]{:S(2)}) %copy-start.2) | copy-done | bytes 524312
  7.6 0.0 copy-start.3
  7.6 1.0 %copy-done.3 = f32[1,1,32,32,128]{4,3,2,1,0:T(8,128)S(1)} copy-done((f32[1,1,32,32,128]{4,3,2,1,0:T(8,128)S(1)}, f32[1,1,32,32,128]{4,3,2,1,0:T(8,128)}, u32[]{:S(2)}) %copy-start.3) | copy-done | bytes 524312
  8.7 0.0 copy-start.4
  8.7 1.0 %copy-done.4 = bf16[256,768]{1,0:T(8,128)(2,1)S(1)} copy-done((bf16[256,768]{1,0:T(8,128)(2,1)S(1)}, bf16[256,768]{1,0:T(8,128)(2,1)}, u32[]{:S(2)}) %copy-start.4) | copy-done | bytes 393240
  9.7 0.0 copy-start.5
  9.7 1.0 %copy-done.5 = f32[17,32,128]{2,1,0:T(8,128)S(1)} copy-done((f32[17,32,128]{2,1,0:T(8,128)S(1)}, f32[17,32,128]{2,1,0:T(8,128)}, u32[]{:S(2)}) %copy-start.5) | copy-done | bytes 278552
  10.6 0.0 copy-start.7
  10.6 0.9 copy-done.7
  11.5 0.0 copy-start.8
  11.5 0.9 copy-done.8
  12.4 0.0 copy-start.9
  12.4 0.9 copy-done.9
  13.3 0.0 copy-start.10
  13.3 0.9 copy-done.10
  14.2 0.0 copy-start.11
  14.2 0.8 copy-done.11
  15.0 75.9 %shard_map.167 = (f32[16,128,128]{2,1,0:T(8,128)S(1)}, f32[1024,128]{1,0:T(8,128)S(1)}) custom-call(f32[256,8,128]{2,1,0:T(8,128)S(1)} %bitcast.16, f32[256,8,128]{2,1,0:T(8,128)S(1)} %bitcast.17, f32[1024,128]{1,0:T(8,128)S(1)} %bitcast.19, f32[1024,128]{1,0:T(8,128)S(1)} %bitcast.20, s32[32]{0:T(128)S(1)} %bitcast.23, s32[32,32]{1,0:T(8,128)S(1)} %bitcast.22, ...), custom_call_target="tpu_custom_call" | custom-call | tf_op jit(solution)/shard_map/pallas_call | solution.py:498
  90.9 1.0 %copy.21 = f32[1,16,128,128]{3,2,1,0:T(8,128)} copy(f32[1,16,128,128]{3,2,1,0:T(8,128)S(1)} %bitcast.18) | data formatting | bytes 2097152
  91.8 0.8 copy.22
Async XLA Ops:
  0.6 2.9 %copy-start.6 = (bf16[384,128]{1,0:T(8,128)(2,1)S(1)}, bf16[384,128]{1,0:T(8,128)(2,1)}, u32[]{:S(2)}) copy-start(bf16[384,128]{1,0:T(8,128)(2,1)} %constant.45.clone.cross_t) | copy-start | bytes 294916
  3.4 0.7 copy-start.12
  3.4 0.7 copy-start.13
  3.4 0.7 copy-start.14
  4.1 1.2 %copy-start = (f32[1,256,8,128]{3,2,1,0:T(8,128)S(1)}, f32[1,256,8,128]{3,2,1,0:T(8,128)}, u32[]{:S(2)}) copy-start(f32[1,256,8,128]{3,2,1,0:T(8,128)} %param.16) | copy-start | bytes 3145732
  5.4 1.2 %copy-start.1 = (f32[1,256,8,128]{3,2,1,0:T(8,128)S(1)}, f32[1,256,8,128]{3,2,1,0:T(8,128)}, u32[]{:S(2)}) copy-start(f32[1,256,8,128]{3,2,1,0:T(8,128)} %param.17) | copy-start | bytes 3145732
  6.6 1.0 %copy-start.2 = (f32[1,1,32,32,128]{4,3,2,1,0:T(8,128)S(1)}, f32[1,1,32,32,128]{4,3,2,1,0:T(8,128)}, u32[]{:S(2)}) copy-start(f32[1,1,32,32,128]{4,3,2,1,0:T(8,128)} %param.18) | copy-start | bytes 1572868
  7.6 1.0 %copy-start.3 = (f32[1,1,32,32,128]{4,3,2,1,0:T(8,128)S(1)}, f32[1,1,32,32,128]{4,3,2,1,0:T(8,128)}, u32[]{:S(2)}) copy-start(f32[1,1,32,32,128]{4,3,2,1,0:T(8,128)} %param.19) | copy-start | bytes 1572868
  8.7 1.0 %copy-start.4 = (bf16[256,768]{1,0:T(8,128)(2,1)S(1)}, bf16[256,768]{1,0:T(8,128)(2,1)}, u32[]{:S(2)}) copy-start(bf16[256,768]{1,0:T(8,128)(2,1)} %constant.39.clone.cosx_t) | copy-start | bytes 1179652
  9.7 1.0 %copy-start.5 = (f32[17,32,128]{2,1,0:T(8,128)S(1)}, f32[17,32,128]{2,1,0:T(8,128)}, u32[]{:S(2)}) copy-start(f32[17,32,128]{2,1,0:T(8,128)} %constant.44.clone.room_t) | copy-start | bytes 835588
  10.6 0.9 copy-start.7
  11.5 0.9 copy-start.8
  12.4 0.9 copy-start.9
  13.3 0.9 copy-start.10
  14.2 0.8 copy-start.11
where the time goes:
time: 93.3 us; the launch traced here: 92.6 us
  Pallas kernels  75.9 us (81%)
  local copies, waits for them, and re-layouts  14 us (15%)
  other arithmetic  2.04 us (2%)
    pallas_call x1, Pallas kernels, local(): pl.pallas_call(functools.partial(kernel, groups, slabs, count), out_shape...  75.9 us
    unnamed x33, local copies, waits for them, and re-layouts  13.7 us

commit v1 on v0

v1 whole, which is shorter than its diff:
```python
import functools
import math

import jax
import jax.numpy as jnp
import ml_dtypes
import numpy as np
from jax import lax
from jax.experimental import pallas as pl
from jax.experimental.pallas import tpu as pltpu
from jax.sharding import PartitionSpec as P

SY = 8
SZ = 16
STEPS = 4
SHORTEST = 16
TIME_STEP = 0.4
SCALE = (TIME_STEP * math.pi) ** 2
STENCIL = np.array([[270, -27, 2], [-27, 2, 0], [2, 0, 0]], np.float64) / 180.0
F32 = jnp.float32
BF16 = jnp.bfloat16
MESH = pl.DeviceIdType.MESH


def dct(length):
    k = np.arange(length)[:, None]
    i = np.arange(length)[None, :]
    w = np.where(k == 0, np.sqrt(1.0 / length), np.sqrt(2.0 / length))
    return w * np.cos(np.pi * k * (2 * i + 1) / (2 * length))


def halves(x):
    high = x.astype(np.float32).astype(ml_dtypes.bfloat16)
    low = (x - high.astype(np.float64)).astype(ml_dtypes.bfloat16)
    return high, low


def left_table(x):
    high, low = halves(x)
    return np.concatenate([high, high, low], axis=1)


def right_table(x):
    high, low = halves(x)
    return np.concatenate([high, high, low], axis=0)


def face_rows(table):
    length = table.shape[0]
    sign = np.where(np.arange(length) % 2 == 0, 1.0, -1.0)
    low = table[:, :3].T
    forced = STENCIL.T @ low
    zero = np.zeros((2, length))
    return (
        np.concatenate([low, low * sign, zero], axis=0),
        np.concatenate([forced, forced * sign, zero], axis=0),
    )


def hall_tables(nx, ny, nz):
    faces, forced = face_rows(dct(nz))
    high, low = halves(faces)
    spread = np.concatenate(
        [np.concatenate([high, high], axis=1), np.concatenate([low, 0 * low], axis=1)], axis=0
    )
    pairs = np.concatenate([forced[k : k + 1] * faces for k in range(6)], axis=0)
    both = np.concatenate(halves(pairs), axis=0)
    respond = np.concatenate(
        [np.concatenate([both, 0 * both], axis=1), np.concatenate([0 * both, both], axis=1)], axis=0
    )
    high, low = halves(forced)
    outer = np.concatenate([high, high, low, low], axis=0)
    blank = np.zeros((32, 384), ml_dtypes.bfloat16)
    outer = np.concatenate([np.concatenate([blank[:, : 128 * t], outer, blank[:, 128 * t :]], axis=1) for t in range(4)], axis=0)
    return spread, respond, outer, left_table(dct(nx).T), left_table(dct(ny).T), right_table(dct(nz))


def room_tables(width):
    faces, forced, full = [], [], []
    for length in range(SHORTEST, width + 1):
        table = np.zeros((width, width))
        table[:length, :length] = dct(length)
        low, high = face_rows(table[:, :])
        faces.append(np.tile(low, (1, 4)))
        forced.append(np.tile(high, (1, 4)))
        full.append(np.tile(table.T, (1, 4)))
    return [np.stack(t).astype(np.float32) for t in (faces, forced, full)]


def factors(q):
    h = jnp.full_like(q, 2.0 / math.factorial(16))
    for n in range(6, -1, -1):
        h = 2.0 / math.factorial(2 * n + 2) - h * q
    return 2.0 - q * h, (TIME_STEP * TIME_STEP) * h


def mm(a, b):
    return jnp.dot(a, b, preferred_element_type=F32)


def mm_nt(a, b):
    return lax.dot_general(a, b, (((1,), (1,)), ((), ())), preferred_element_type=F32)


def split(x):
    high = x.astype(BF16)
    return high, (x - high.astype(F32)).astype(BF16)


def stacked(x, axis):
    high, low = split(x)
    return jnp.concatenate([high, low, high], axis=axis)


def lane_tiles(table):
    if table.shape[1] == 128:
        return table
    tile = math.gcd(table.shape[1], 128)
    return table.reshape(table.shape[0], -1, tile).transpose(1, 0, 2)


def broad(ref, tiles=None, rows=None):
    tiles = ref.shape[0] if tiles is None else tiles
    return jnp.concatenate([ref[j, :rows] for j in range(tiles)], axis=1)


def iota(shape, dim):
    return lax.broadcasted_iota(jnp.int32, shape, dim).astype(F32)


def total(mask, values, axis):
    return jnp.sum(jnp.where(mask, values, 0.0), axis=axis, keepdims=True)


def kernel(
    groups, slabs, count, loads, *refs,
):
    lengths, sources, refs = refs[0], refs[1 : 1 + loads], refs[1 + loads :]
    hall_out, room_out = refs[:2]
    landed, refs = refs[2 : 2 + loads], refs[2 + loads :]
    (
        hall_now, hall_prev, room_now, room_prev, ids,
        spread_t, respond_t, outer_t, cosx_t, cosy_t, cosz_t, face_t, force_t, room_t, cross_t,
    ) = landed
    (
        hall_c2, hall_gain, hall_base, hall_faces, hall_resp, hall_diff, hall_other,
        hall_send, hall_recv, a2a_send, a2a_recv,
        room_c2, room_gain, room_a, room_b, room_faces, raw_faces, raw_force, raw_full,
        face_l, force_l, full_l, pack_l, take_l, room_send, room_recv,
        load_sem, hall_ssem, hall_rsem, a2a_ssem, a2a_rsem, room_ssem, room_rsem,
    ) = refs
    me = lax.axis_index("grp")
    column = lax.axis_index("slab")
    nx, part_y, nz = hall_now.shape
    ny = part_y * slabs
    part_x = nx // slabs
    lanes = nx * part_y
    width = room_now.shape[0] // count
    batches = count // 4

    copies = [pltpu.make_async_copy(sources[i], landed[i], load_sem.at[i]) for i in range(loads)]
    order = [0, 5, 2, 4, 11, 1, 6, 3, 12, 7, 13, 8, 10, 9, 14]
    for i in order:
        copies[i].start()

    barrier = pltpu.get_barrier_semaphore()

    def greet_grp(step, carry):
        pl.semaphore_signal(
            barrier, inc=1, device_id=(lax.rem(me + step, groups), column), device_id_type=MESH
        )
        return carry

    def greet_slab(step, carry):
        pl.semaphore_signal(
            barrier, inc=1, device_id=(me, lax.rem(column + step, slabs)), device_id_type=MESH
        )
        return carry

    lax.fori_loop(1, groups, greet_grp, 0)
    lax.fori_loop(1, slabs, greet_slab, 0)
    hall_other[...] = jnp.zeros_like(hall_other)

    chunk = 256
    deep = chunk // part_y

    def spread_of(x):
        high, low = split(x)
        both = mm_nt(broad(spread_t), jnp.concatenate([high, low], axis=1))
        return both[:8] + both[8:]

    def first_faces(i, carry):
        x = hall_now[pl.ds(i * deep, deep)].reshape(chunk, nz)
        hall_faces[0, :, pl.ds(pl.multiple_of(i * chunk, chunk), chunk)] = spread_of(x)
        return carry

    copies[0].wait()
    copies[5].wait()
    lax.fori_loop(0, lanes // chunk, first_faces, 0)

    def hall_copy(t, side):
        peer = lax.rem(me + (1 if side == 0 else groups - 1), groups)
        return pltpu.make_async_remote_copy(
            src_ref=hall_send.at[t, side],
            dst_ref=hall_recv.at[t, side],
            send_sem=hall_ssem.at[t, side],
            recv_sem=hall_rsem.at[t, side],
            device_id=(peer, column),
            device_id_type=MESH,
        )

    def hall_put(t):
        own = hall_faces[t]
        for k in range(3):
            for j in range(lanes // 128):
                cut = slice(128 * j, 128 * j + 128)
                hall_send[t, 0, k, j : j + 1, :] = own[3 + k : 4 + k, cut]
                hall_send[t, 1, k, j : j + 1, :] = own[k : k + 1, cut]
        hall_copy(t, 0).start()
        hall_copy(t, 1).start()

    def hall_get(t):
        hall_copy(t, 0).wait_recv()
        hall_copy(t, 1).wait_recv()
        for k in range(3):
            for j in range(lanes // 128):
                cut = slice(128 * j, 128 * j + 128)
                hall_other[k : k + 1, cut] = hall_recv[t, 0, k, j : j + 1, :]
                hall_other[3 + k : 4 + k, cut] = hall_recv[t, 1, k, j : j + 1, :]
        row = lax.broadcasted_iota(jnp.int32, (8, lanes), 0)
        first = jnp.where(me > 0, 0, 3)
        last = jnp.where(me < groups - 1, 6, 3)
        diff = jnp.where((row >= first) & (row < last), hall_other[...] - hall_faces[t], 0.0)
        hall_diff[t] = diff
        return diff

    def hall_respond(t, lag, diff):
        acc = hall_faces[t + lag]
        for k in range(6):
            acc = acc + hall_resp[lag - 1, 8 * k : 8 * k + 8, :] * diff[k : k + 1, :]
        hall_faces[t + lag] = acc

    def terms(e):
        high = e.astype(BF16).astype(F32)
        low = e - high
        return jnp.concatenate([high, low, high, low], axis=0)

    def accumulate_early(i, carry):
        at = pl.ds(i * deep, deep)
        cols = pl.ds(pl.multiple_of(i * chunk, chunk), chunk)
        e = jnp.concatenate([terms(hall_diff[t, :, cols]) for t in range(3)], axis=0).T.astype(BF16)
        forced = mm(e, broad(outer_t, 3, 96))
        c2 = hall_c2[at]
        f0, f1, f2 = [forced[:, 128 * t : 128 * t + 128].reshape(deep, part_y, nz) for t in range(3)]
        square = c2 * c2
        weighted = c2 * ((square - 2.0) * f0 + f2) + (square - 1.0) * f1
        hall_base[at] = hall_base[at] + hall_gain[at] * weighted
        return carry

    def accumulate_last(i, carry):
        at = pl.ds(i * deep, deep)
        cols = pl.ds(pl.multiple_of(i * chunk, chunk), chunk)
        e = terms(hall_diff[3, :, cols]).T.astype(BF16)
        forced = mm(e, outer_t[0, :32]).reshape(deep, part_y, nz)
        hall_base[at] = hall_base[at] + hall_gain[at] * forced
        return carry

    pl.semaphore_wait(barrier, groups + slabs - 2)
    hall_put(0)

    lane = lax.broadcasted_iota(jnp.int32, (width, 128), 1)
    kx = lax.broadcasted_iota(jnp.int32, (width, 128), 0)

    def room_first(b, carry):
        for i in range(4):
            r = 4 * b + i
            length = lengths[0, 0, r]
            which = jnp.maximum(length - SHORTEST, 0)
            at = pl.ds(pl.multiple_of(r * width, width), width)
            at8 = pl.ds(pl.multiple_of(r * 8, 8), 8)
            mine = lane // width == i
            raw_faces[at8, :] = jnp.where(mine[:8], face_t[which], 0.0)
            room_a[at, :] = jnp.where(kx < jnp.full((width, 128), length, jnp.int32), room_now[at, :], 0.0)
        return carry

    copies[2].wait()
    copies[4].wait()
    copies[11].wait()
    lax.fori_loop(0, batches, room_first, 0)
    for b in range(batches):
        cut = slice(32 * b, 32 * b + 32)
        big = slice(128 * b, 128 * b + 128)
        high, low = split(raw_faces[cut, :])
        face_l[cut, :] = jnp.concatenate([high, high, low], axis=1)
        room_faces[cut, :] = mm(face_l[cut, :], stacked(room_a[big, :], 0))

    bits = int(math.log2(count))
    wide = 8 * count
    span = ids.shape[1]
    row_lanes = min(128, span)
    flat = jnp.concatenate(
        [ids[0:1, row_lanes * j : row_lanes * (j + 1)] for j in range(span // row_lanes)], axis=0
    )
    device = (flat >> bits).astype(F32)
    slot = (flat & (count - 1)).astype(F32)
    lane_i = lax.broadcasted_iota(jnp.int32, (count, wide), 1)
    p_col = iota((count, wide), 0)
    p_row = (lane_i >> 3).astype(F32)
    f_row = (lane_i & 7).astype(F32)
    expand = lax.broadcasted_iota(jnp.int32, (row_lanes, wide), 1) >> 3
    expand = jnp.where(expand == lax.broadcasted_iota(jnp.int32, (row_lanes, wide), 0), 1.0, 0.0)
    s_row = mm(device.astype(BF16), expand.astype(BF16))[0:1]
    s_col = device.T[:count, 0:1]
    same = s_col == s_row
    rank_row = total(same & (p_col < p_row), 1.0, 0)
    rank_col = total(same & (p_row < p_col) & (f_row == 0.0), 1.0, 1)
    home = me.astype(F32) - s_col
    home = jnp.where(home < 0.0, home + groups, home)
    per_row = row_lanes // count
    home = jnp.concatenate([home] * per_row, axis=0)
    shape = (row_lanes, span // row_lanes)
    group = per_row * lax.broadcasted_iota(jnp.int32, shape, 1)
    group = group + (lax.broadcasted_iota(jnp.int32, shape, 0) >> bits)
    landing = total(group.astype(F32) == home, slot.T, 1)
    landing = sum(landing[count * i : count * (i + 1)] for i in range(per_row))
    match = landing == p_row
    ls_row = total(match, jnp.broadcast_to(s_col, (count, wide)), 0)
    lr_row = total(match, jnp.broadcast_to(rank_col, (count, wide)), 0)

    def back(s):
        return jnp.where(s == 0.0, 0.0, groups - s)

    f = f_row[0:1]
    layer = jnp.where(f < 3.0, f, f - 3.0)
    pack_row = jnp.where(
        f < 3.0, 16.0 * back(ls_row) + 6.0 + 3.0 * lr_row + layer, 16.0 * s_row + 3.0 * rank_row + layer
    )
    take_row = jnp.where(
        f < 3.0, 16.0 * ls_row + 3.0 * lr_row + layer, 16.0 * back(s_row) + 6.0 + 3.0 * rank_row + layer
    )
    pack_row = jnp.where(f < 6.0, pack_row, -1.0)
    take_row = jnp.where(f < 6.0, take_row, -1.0)
    slots = 16 * groups
    pack_l[...] = jnp.where(iota((slots, wide), 0) == pack_row, 1.0, 0.0).astype(BF16)

    def room_copy(t, step):
        return pltpu.make_async_remote_copy(
            src_ref=room_send.at[t, step],
            dst_ref=room_recv.at[t, step - 1],
            send_sem=room_ssem.at[t, step - 1],
            recv_sem=room_rsem.at[t, step - 1],
            device_id=(lax.rem(me + step, groups), column),
            device_id_type=MESH,
        )

    def far_first(i, count):
        half = i // 2
        return count // 2 + jnp.where(lax.rem(i, 2) == 0, half, -half)

    def two_parts(x):
        return jnp.concatenate(split(x), axis=1)

    def room_put(t):
        packed = mm(pack_l[...], two_parts(room_faces[...]))
        packed = packed[:, :128] + packed[:, 128:]
        room_send[t] = packed.reshape(groups, 16, 128)[:, :12, :]

        def body(i, carry):
            room_copy(t, far_first(i, groups)).start()
            return carry

        lax.fori_loop(1, groups, body, 0)

    def room_get(t):
        def body(i, carry):
            room_copy(t, far_first(i, groups)).wait_recv()
            return carry

        lax.fori_loop(1, groups, body, 0)
        got = jnp.concatenate([room_send[t, 0:1], room_recv[t]], axis=0)
        got = jnp.concatenate([got, jnp.zeros((groups, 4, 128), F32)], axis=1).reshape(slots, 128)
        other = mm(take_l[...], two_parts(got))
        return other[:, :128] + other[:, 128:] - room_faces[...]

    def room_sent(t):
        def body(step, carry):
            room_copy(t, step).wait_send()
            return carry

        lax.fori_loop(1, groups, body, 0)

    def room_step(t):
        diff = room_get(t)
        now, prev = (room_a, room_b) if t % 2 == 0 else (room_b, room_a)
        for b in range(batches):
            cut = slice(32 * b, 32 * b + 32)
            big = slice(128 * b, 128 * b + 128)
            high, low = split(diff[cut])
            forced = mm(force_l[big, :], jnp.concatenate([high, low, high, low], axis=0))
            fresh = room_c2[big, :] * now[big, :] - prev[big, :] + room_gain[big, :] * forced
            if t < STEPS - 1:
                prev[big, :] = fresh
                room_faces[cut, :] = mm(face_l[cut, :], stacked(fresh, 0))
            else:
                x = mm(full_l[big, :], stacked(fresh, 0))
                room_out[big, :] = mm(stacked(x, 1), cross_t[...])
        if t < STEPS - 1:
            room_put(t + 1)
            room_sent(t)

    room_put(0)

    yz = lax.broadcasted_iota(jnp.int32, (part_y, nz), 0) + column * part_y
    ky_f = yz.astype(F32)
    kz_f = iota((part_y, nz), 1)
    q_yz = (SCALE / ny**2) * (ky_f * ky_f) + (SCALE / nz**2) * (kz_f * kz_f)

    def prepare_first(i, carry):
        at = pl.ds(i * deep, deep)
        cols = pl.ds(pl.multiple_of(i * chunk, chunk), chunk)
        a = (lax.broadcasted_iota(jnp.int32, (deep, part_y, nz), 0) + i * deep).astype(F32)
        c2, gain = factors((SCALE / nx**2) * (a * a) + q_yz[None])
        hall_c2[at] = c2
        hall_gain[at] = gain
        fresh = c2 * hall_now[at] - hall_prev[at]
        hall_base[at] = fresh
        hall_faces[1, :, cols] = spread_of(fresh.reshape(chunk, nz))
        both = mm_nt(respond_t[0, :96], gain.reshape(chunk, nz).astype(BF16))
        hall_resp[0, :, cols] = both[:48] + both[48:]
        return carry

    def prepare_last(i, carry):
        at = pl.ds(i * deep, deep)
        cols = pl.ds(pl.multiple_of(i * chunk, chunk), chunk)
        c2 = hall_c2[at]
        gain = hall_gain[at]
        m1 = hall_base[at]
        m2 = c2 * m1 - hall_now[at]
        m3 = c2 * m2 - m1
        hall_base[at] = c2 * m3 - m2
        hall_faces[2, :, cols] = spread_of(m2.reshape(chunk, nz))
        hall_faces[3, :, cols] = spread_of(m3.reshape(chunk, nz))
        s2 = gain * c2
        s3 = s2 * c2 - gain
        both = [s.reshape(chunk, nz).astype(BF16) for s in (s2, s3)]
        both = mm_nt(broad(respond_t), jnp.concatenate(both, axis=1))
        hall_resp[1, :, cols] = both[:48] + both[48:96]
        hall_resp[2, :, cols] = both[96:144] + both[144:]
        return carry

    copies[1].wait()
    copies[6].wait()
    lax.fori_loop(0, lanes // chunk, prepare_first, 0)
    diff = hall_get(0)
    hall_respond(0, 1, diff)
    hall_put(1)
    lax.fori_loop(0, lanes // chunk, prepare_last, 0)
    hall_respond(0, 2, diff)
    hall_respond(0, 3, diff)
    diff = hall_get(1)
    hall_respond(1, 1, diff)
    hall_put(2)
    hall_respond(1, 2, diff)

    q_cross = (lane // SZ).astype(F32) / SY
    q_cross = SCALE * (q_cross * q_cross)
    z_part = (lane % SZ).astype(F32) / SZ
    q_cross = q_cross + SCALE * (z_part * z_part)
    kx_f = kx.astype(F32)
    kx_sq = SCALE * (kx_f * kx_f)

    def room_second(b, carry):
        for i in range(4):
            r = 4 * b + i
            length = lengths[0, 0, r]
            which = jnp.maximum(length - SHORTEST, 0)
            at = pl.ds(pl.multiple_of(r * width, width), width)
            at8 = pl.ds(pl.multiple_of(r * 8, 8), 8)
            mine = lane // width == i
            raw_force[at8, :] = jnp.where(mine[:8], force_t[which], 0.0)
            extent = jnp.full((width, 128), length, jnp.int32)
            live = kx < extent
            extent = extent.astype(F32)
            c2, gain = factors(kx_sq / (extent * extent) + q_cross)
            room_c2[at, :] = c2
            room_gain[at, :] = gain
            room_b[at, :] = jnp.where(live, room_prev[at, :], 0.0)
        return carry

    copies[3].wait()
    copies[12].wait()
    copies[7].wait()
    lax.fori_loop(0, batches, room_second, 0)
    for b in range(batches):
        x = raw_force[32 * b : 32 * b + 32, :]
        high = x.astype(BF16).astype(F32)
        low = x - high
        force_l[128 * b : 128 * b + 128, :] = jnp.concatenate([high, high, low, low], axis=0).T.astype(BF16)
    take_col = jnp.broadcast_to(take_row, (8, wide)).T[:, 0:1]
    take_l[...] = jnp.where(iota((wide, slots), 1) == take_col, 1.0, 0.0).astype(BF16)

    diff = hall_get(2)
    hall_respond(2, 1, diff)
    hall_put(3)
    room_step(0)
    lax.fori_loop(0, lanes // chunk, accumulate_early, 0)
    hall_get(3)
    lax.fori_loop(0, lanes // chunk, accumulate_last, 0)

    parts = 2
    part_b = part_y // parts

    def a2a_copy(h, step):
        peer = lax.rem(column + step, slabs)
        return pltpu.make_async_remote_copy(
            src_ref=a2a_send.at[pl.ds(part_b * h, part_b), pl.ds(pl.multiple_of(peer * part_x, part_x), part_x), :],
            dst_ref=a2a_recv.at[pl.ds(column * part_y + part_b * h, part_b)],
            send_sem=a2a_ssem.at[h, step],
            recv_sem=a2a_rsem.at[h, step],
            device_id=(me, peer),
            device_id_type=MESH,
        )

    copies[8].wait()
    for h in range(parts):
        for b in range(part_b * h, part_b * h + part_b, 2):
            pair = [stacked(hall_base[:, b + i, :], 0) for i in range(2)]
            y = mm(broad(cosx_t), jnp.concatenate(pair, axis=1))
            a2a_send[b] = y[:, :nz]
            a2a_send[b + 1] = y[:, nz:]

        def a2a_start(i, carry):
            a2a_copy(h, far_first(i, slabs)).start()
            return carry

        lax.fori_loop(1, slabs, a2a_start, 0)

    def z_part_of(x):
        x = stacked(x.reshape(part_y * part_x, nz), 1)
        return mm(x, cosz_t[...]).reshape(part_y, part_x, nz)

    copies[10].wait()
    own = pl.ds(pl.multiple_of(column * part_x, part_x), part_x)
    a2a_recv[pl.ds(column * part_y, part_y)] = z_part_of(a2a_send[:, own, :])

    def a2a_take(i, carry):
        step = far_first(i, slabs)
        a2a_copy(0, step).wait_recv()
        a2a_copy(1, step).wait_recv()
        source = lax.rem(column + slabs - step, slabs)
        at = pl.ds(source * part_y, part_y)
        a2a_recv[at] = z_part_of(a2a_recv[at])
        return carry

    def room_tables_full(b, carry):
        for i in range(4):
            r = 4 * b + i
            which = jnp.maximum(lengths[0, 0, r] - SHORTEST, 0)
            at = pl.ds(pl.multiple_of(r * width, width), width)
            raw_full[at, :] = jnp.where(lane // width == i, room_t[which], 0.0)
        return carry

    copies[13].wait()
    copies[14].wait()
    lax.fori_loop(0, batches, room_tables_full, 0)
    for b in range(batches):
        big = slice(128 * b, 128 * b + 128)
        high, low = split(raw_full[big, :])
        full_l[big, :] = jnp.concatenate([high, high, low], axis=1)

    room_step(1)
    for t in range(STEPS - 1):
        hall_copy(t, 0).wait_send()
        hall_copy(t, 1).wait_send()
    room_step(2)
    hall_copy(3, 0).wait_send()
    hall_copy(3, 1).wait_send()
    room_step(3)
    room_sent(3)
    lax.fori_loop(1, slabs, a2a_take, 0)
    copies[9].wait()
    for x in range(0, part_x, 2):
        pair = jnp.concatenate([stacked(a2a_recv[:, x, :], 0), stacked(a2a_recv[:, x + 1, :], 0)], axis=1)
        y = mm(broad(cosy_t), pair)
        hall_out[x] = y[:, :nz]
        hall_out[x + 1] = y[:, nz:]

    def a2a_sent(step, carry):
        a2a_copy(0, step).wait_send()
        a2a_copy(1, step).wait_send()
        return carry

    lax.fori_loop(1, slabs, a2a_sent, 0)


def local(hall_now, hall_prev, room_now, room_prev, room_length, right_neighbor):
    groups = lax.axis_size("grp")
    slabs = lax.axis_size("slab")
    _, nx, part_y, nz = hall_now.shape
    _, _, count, width, cross = room_now.shape
    ny = part_y * slabs
    part_x = nx // slabs
    lanes = nx * part_y
    slots = 16 * groups
    rows = count * width
    inputs = [
        hall_now[0], hall_prev[0], room_now.reshape(rows, cross), room_prev.reshape(rows, cross), right_neighbor,
    ]
    inputs += [jnp.asarray(lane_tiles(t)) for t in hall_tables(nx, ny, nz)]
    inputs += [jnp.asarray(t) for t in room_tables(width)]
    inputs += [jnp.asarray(right_table(np.kron(dct(SY), dct(SZ))))]
    vmem = pl.BlockSpec(memory_space=pltpu.VMEM)
    smem = pl.BlockSpec(memory_space=pltpu.SMEM)
    away = pl.BlockSpec(memory_space=pl.ANY)
    dma = pltpu.SemaphoreType.DMA
    hall_pressure, room_pressure = pl.pallas_call(
        functools.partial(kernel, groups, slabs, count, len(inputs)),
        out_shape=(
            jax.ShapeDtypeStruct((part_x, ny, nz), F32),
            jax.ShapeDtypeStruct((rows, cross), F32),
        ),
        in_specs=[smem] + [away] * len(inputs),
        out_specs=(vmem, vmem),
        scratch_shapes=[pltpu.VMEM(x.shape, x.dtype) for x in inputs]
        + [
            pltpu.VMEM((nx, part_y, nz), F32),
            pltpu.VMEM((nx, part_y, nz), F32),
            pltpu.VMEM((nx, part_y, nz), F32),
            pltpu.VMEM((STEPS, 8, lanes), F32),
            pltpu.VMEM((STEPS - 1, 48, lanes), F32),
            pltpu.VMEM((STEPS, 8, lanes), F32),
            pltpu.VMEM((8, lanes), F32),
            pltpu.VMEM((STEPS, 2, 3, lanes // 128, 128), F32),
            pltpu.VMEM((STEPS, 2, 3, lanes // 128, 128), F32),
            pltpu.VMEM((part_y, nx, nz), F32),
            pltpu.VMEM((ny, part_x, nz), F32),
            pltpu.VMEM((rows, cross), F32),
            pltpu.VMEM((rows, cross), F32),
            pltpu.VMEM((rows, cross), F32),
            pltpu.VMEM((rows, cross), F32),
            pltpu.VMEM((8 * count, cross), F32),
            pltpu.VMEM((8 * count, 4 * width), F32),
            pltpu.VMEM((8 * count, 4 * width), F32),
            pltpu.VMEM((rows, 4 * width), F32),
            pltpu.VMEM((8 * count, 12 * width), BF16),
            pltpu.VMEM((rows, 128), BF16),
            pltpu.VMEM((rows, 12 * width), BF16),
            pltpu.VMEM((slots, 8 * count), BF16),
            pltpu.VMEM((8 * count, slots), BF16),
            pltpu.VMEM((STEPS, groups, 12, 128), F32),
            pltpu.VMEM((STEPS, groups - 1, 12, 128), F32),
            dma((len(inputs),)),
            dma((STEPS, 2)),
            dma((STEPS, 2)),
            dma((2, slabs)),
            dma((2, slabs)),
            dma((STEPS, groups - 1)),
            dma((STEPS, groups - 1)),
        ],
        compiler_params=pltpu.CompilerParams(
            collective_id=0, has_side_effects=True, vmem_limit_bytes=60 * 1024 * 1024
        ),
    )(room_length, *inputs)
    return (hall_pressure[None], room_pressure.reshape(1, 1, count, width, cross))


def solution(mesh):
    in_specs = (
        P("grp", None, "slab", None),
        P("grp", None, "slab", None),
        P("grp", "slab", None, None, None),
        P("grp", "slab", None, None, None),
        P("grp", "slab", None),
        P("slab", None),
    )
    out_specs = (P("grp", "slab", None, None), P("grp", "slab", None, None, None))
    return jax.shard_map(local, mesh=mesh, in_specs=in_specs, out_specs=out_specs, check_vma=False)
```

time: 93.3 us -> 76.2 us (0.82)
  local copies, waits for them, and re-layouts: 14 us -> 3.15 us
  Pallas kernels: 75.9 us -> 72.2 us
  other arithmetic: 2.04 us -> 0 us
    unnamed x33 -> x4, local copies, waits for them, and re-layouts: 13.7 us -> 3.15 us
    pallas_call x1, Pallas kernels: 75.9 us -> 72.2 us  [local(): pl.pallas_call(functools.partial(kernel, groups, slabs, count, len(inputs...]
    unnamed x1 -> x0, other arithmetic: 1.35 us -> none
where the time goes in v1:
time: 76.2 us; the launch traced here: 76 us
  Pallas kernels  72.2 us (95%)
  local copies, waits for them, and re-layouts  3.15 us (4%)
    pallas_call x1, Pallas kernels, local(): pl.pallas_call(functools.partial(kernel, groups, slabs, count, len(inputs...  72.2 us
    unnamed x4, local copies, waits for them, and re-layouts  3.15 us

profile of v1, /device:TPU:1, one launch (start us, length us, event | category | flops | bytes accessed | tf_op | source)
XLA Modules:
  0.0 76.0 jit_solution(12073072052471841425)
XLA Ops:
  0.6 72.2 %shard_map.167 = (f32[16,128,128]{2,1,0:T(8,128)}, f32[1024,128]{1,0:T(8,128)}) custom-call(s32[1,1,32]{2,1,0:T(1,128)} %refs_0_.1, f32[256,8,128]{2,1,0:T(8,128)} %bitcast.7, f32[256,8,128]{2,1,0:T(8,128)} %bitcast.8, f32[1024,128]{1,0:T(8,128)} %bitcast.10, f32[1024,128]{1,0:T(8,128)} %bitcast.11, s32[1,1024]{1,0:T(1,128)} %refs_5_.1, ...), custom_call_target="tpu_custom_call" | custom-call | tf_op jit(solution)/shard_map/pallas_call | solution.py:616
  72.9 0.0 copy-start
  72.9 2.4 %copy.20 = f32[1,16,128,128]{3,2,1,0:T(8,128)} copy(f32[1,16,128,128]{3,2,1,0:T(8,128)} %bitcast.6) | data formatting | bytes 2097152
  75.2 0.0 copy-done
  75.2 0.8 %copy.21 = f32[1,1,32,32,128]{4,3,2,1,0:T(8,128)} copy(f32[1,1,32,32,128]{4,3,2,1,0:T(8,128)S(1)} %bitcast.9) | data formatting | bytes 1048576
Async XLA Ops:
  72.9 2.4 %copy-start = (f32[1024,128]{1,0:T(8,128)S(1)}, f32[1024,128]{1,0:T(8,128)}, u32[]{:S(2)}) copy-start(f32[1024,128]{1,0:T(8,128)} %get-tuple-element.5) | copy-start | bytes 1572868

commit v2 on v1

--- a/solution.py
+++ b/solution.py
@@ -136,7 +136,7 @@
     groups, slabs, count, loads, *refs,
 ):
     lengths, sources, refs = refs[0], refs[1 : 1 + loads], refs[1 + loads :]
-    hall_out, room_out = refs[:2]
+    hall_far, room_far = refs[:2]
     landed, refs = refs[2 : 2 + loads], refs[2 + loads :]
     (
         hall_now, hall_prev, room_now, room_prev, ids,
@@ -146,8 +146,8 @@
         hall_c2, hall_gain, hall_base, hall_faces, hall_resp, hall_diff, hall_other,
         hall_send, hall_recv, a2a_send, a2a_recv,
         room_c2, room_gain, room_a, room_b, room_faces, raw_faces, raw_force, raw_full,
-        face_l, force_l, full_l, pack_l, take_l, room_send, room_recv,
-        load_sem, hall_ssem, hall_rsem, a2a_ssem, a2a_rsem, room_ssem, room_rsem,
+        face_l, force_l, full_l, pack_l, take_l, room_send, room_recv, hall_out, room_out,
+        load_sem, store_sem, hall_ssem, hall_rsem, a2a_ssem, a2a_rsem, room_ssem, room_rsem,
     ) = refs
     me = lax.axis_index("grp")
     column = lax.axis_index("slab")
@@ -371,6 +371,12 @@
 
         lax.fori_loop(1, groups, body, 0)
 
+    def store(which, i):
+        near, far = ((hall_out, hall_far), (room_out, room_far))[which]
+        size = near.shape[0] // (8 if which == 0 else batches)
+        at = pl.ds(i * size, size)
+        return pltpu.make_async_copy(near.at[at], far.at[at], store_sem.at[which, i])
+
     def room_get(t):
         def body(i, carry):
             room_copy(t, far_first(i, groups)).wait_recv()
@@ -404,6 +410,7 @@
             else:
                 x = mm(full_l[big, :], stacked(fresh, 0))
                 room_out[big, :] = mm(stacked(x, 1), cross_t[...])
+                store(1, b).start()
         if t < STEPS - 1:
             room_put(t + 1)
             room_sent(t)
@@ -575,8 +582,6 @@
     room_step(2)
     hall_copy(3, 0).wait_send()
     hall_copy(3, 1).wait_send()
-    room_step(3)
-    room_sent(3)
     lax.fori_loop(1, slabs, a2a_take, 0)
     copies[9].wait()
     for x in range(0, part_x, 2):
@@ -584,6 +589,11 @@
         y = mm(broad(cosy_t), pair)
         hall_out[x] = y[:, :nz]
         hall_out[x + 1] = y[:, nz:]
+    for i in range(8):
+        store(0, i).start()
+
+    room_step(3)
+    room_sent(3)
 
     def a2a_sent(step, carry):
         a2a_copy(0, step).wait_send()
@@ -591,6 +601,23 @@
         return carry
 
     lax.fori_loop(1, slabs, a2a_sent, 0)
+    for i in range(8):
+        store(0, i).wait()
+    for i in range(batches):
+        store(1, i).wait()
+
+
+def hand_on(hall_in, room_in, hall_out, room_out, sem):
+    copies = []
+    for j, (near, far) in enumerate(((hall_in, hall_out), (room_in, room_out))):
+        size = near.shape[0] // 8
+        for i in range(8):
+            at = pl.ds(i * size, size)
+            copies.append(pltpu.make_async_copy(near.at[at], far.at[at], sem.at[j, i]))
+    for copy in copies:
+        copy.start()
+    for copy in copies:
+        copy.wait()
 
 
 def local(hall_now, hall_prev, room_now, room_prev, room_length, right_neighbor):
@@ -609,18 +636,17 @@
     inputs += [jnp.asarray(lane_tiles(t)) for t in hall_tables(nx, ny, nz)]
     inputs += [jnp.asarray(t) for t in room_tables(width)]
     inputs += [jnp.asarray(right_table(np.kron(dct(SY), dct(SZ))))]
-    vmem = pl.BlockSpec(memory_space=pltpu.VMEM)
     smem = pl.BlockSpec(memory_space=pltpu.SMEM)
     away = pl.BlockSpec(memory_space=pl.ANY)
     dma = pltpu.SemaphoreType.DMA
-    hall_pressure, room_pressure = pl.pallas_call(
+    results = pl.pallas_call(
         functools.partial(kernel, groups, slabs, count, len(inputs)),
         out_shape=(
             jax.ShapeDtypeStruct((part_x, ny, nz), F32),
             jax.ShapeDtypeStruct((rows, cross), F32),
         ),
         in_specs=[smem] + [away] * len(inputs),
-        out_specs=(vmem, vmem),
+        out_specs=(away, away),
         scratch_shapes=[pltpu.VMEM(x.shape, x.dtype) for x in inputs]
         + [
             pltpu.VMEM((nx, part_y, nz), F32),
@@ -649,7 +675,10 @@
             pltpu.VMEM((8 * count, slots), BF16),
             pltpu.VMEM((STEPS, groups, 12, 128), F32),
             pltpu.VMEM((STEPS, groups - 1, 12, 128), F32),
+            pltpu.VMEM((part_x, ny, nz), F32),
+            pltpu.VMEM((rows, cross), F32),
             dma((len(inputs),)),
+            dma((2, 8)),
             dma((STEPS, 2)),
             dma((STEPS, 2)),
             dma((2, slabs)),
@@ -661,6 +690,14 @@
             collective_id=0, has_side_effects=True, vmem_limit_bytes=60 * 1024 * 1024
         ),
     )(room_length, *inputs)
+    hall_pressure, room_pressure = pl.pallas_call(
+        hand_on,
+        out_shape=tuple(jax.ShapeDtypeStruct(x.shape, x.dtype) for x in results),
+        in_specs=[away] * 2,
+        out_specs=(away, away),
+        scratch_shapes=[dma((2, 8))],
+        compiler_params=pltpu.CompilerParams(vmem_limit_bytes=60 * 1024 * 1024),
+    )(*results)
     return (hall_pressure[None], room_pressure.reshape(1, 1, count, width, cross))
 
 

time: 76.2 us -> 125 us (1.64)
  Pallas kernels: 72.2 us -> 124 us
  local copies, waits for them, and re-layouts: 3.15 us -> 0 us
    pallas_call x0 -> x1, Pallas kernels: none -> 48.9 us  [local(): pl.pallas_call(hand_on, out_shape=tuple((jax.ShapeDtypeStruct(x.shape, x....]
    unnamed x4 -> x0, local copies, waits for them, and re-layouts: 3.15 us -> none
    pallas_call x1, Pallas kernels: 72.2 us -> 75 us  [local(): pl.pallas_call(functools.partial(kernel, groups, slabs, count, len(inputs...]
where the time goes in v2:
time: 125 us
  Pallas kernels  124 us (99%)
    pallas_call x1, Pallas kernels, local(): pl.pallas_call(functools.partial(kernel, groups, slabs, count, len(inputs...  75 us
    pallas_call x1, Pallas kernels, local(): pl.pallas_call(hand_on, out_shape=tuple((jax.ShapeDtypeStruct(x.shape, x....  48.9 us

profile of v2, /device:TPU:1, one launch (start us, length us, event | category | flops | bytes accessed | tf_op | source)
XLA Modules:
  0.0 124.6 jit_solution(16788925865703123458)
XLA Ops:
  0.6 75.0 %shard_map.167 = (f32[16,128,128]{2,1,0:T(8,128)}, f32[1024,128]{1,0:T(8,128)}) custom-call(s32[1,1,32]{2,1,0:T(1,128)} %refs_0_.1, f32[256,8,128]{2,1,0:T(8,128)} %bitcast.6, f32[256,8,128]{2,1,0:T(8,128)} %bitcast.7, f32[1024,128]{1,0:T(8,128)} %bitcast.8, f32[1024,128]{1,0:T(8,128)} %bitcast.9, s32[1,1024]{1,0:T(1,128)} %refs_5_.1, ...), custom_call_target="tpu_custom_call" | custom-call | tf_op jit(solution)/shard_map/pallas_call | solution.py:642
  75.7 48.9 %shard_map.168 = (f32[16,128,128]{2,1,0:T(8,128)}, f32[1024,128]{1,0:T(8,128)}) custom-call(f32[16,128,128]{2,1,0:T(8,128)} %get-tuple-element.6.hall_in, f32[1024,128]{1,0:T(8,128)} %get-tuple-element.7.room_in), custom_call_target="tpu_custom_call" | custom-call | tf_op jit(solution)/shard_map/pallas_call | solution.py:693

commit v3 on v2

--- a/solution.py
+++ b/solution.py
@@ -184,19 +184,26 @@
     chunk = 256
     deep = chunk // part_y
 
+    def chunks(body, many):
+        def several(i, carry):
+            for j in range(many):
+                body(i * many + j)
+            return carry
+
+        lax.fori_loop(0, lanes // chunk // many, several, 0)
+
     def spread_of(x):
         high, low = split(x)
         both = mm_nt(broad(spread_t), jnp.concatenate([high, low], axis=1))
         return both[:8] + both[8:]
 
-    def first_faces(i, carry):
+    def first_faces(i):
         x = hall_now[pl.ds(i * deep, deep)].reshape(chunk, nz)
         hall_faces[0, :, pl.ds(pl.multiple_of(i * chunk, chunk), chunk)] = spread_of(x)
-        return carry
 
     copies[0].wait()
     copies[5].wait()
-    lax.fori_loop(0, lanes // chunk, first_faces, 0)
+    chunks(first_faces, 4)
 
     def hall_copy(t, side):
         peer = lax.rem(me + (1 if side == 0 else groups - 1), groups)
@@ -245,7 +252,7 @@
         low = e - high
         return jnp.concatenate([high, low, high, low], axis=0)
 
-    def accumulate_early(i, carry):
+    def accumulate_early(i):
         at = pl.ds(i * deep, deep)
         cols = pl.ds(pl.multiple_of(i * chunk, chunk), chunk)
         e = jnp.concatenate([terms(hall_diff[t, :, cols]) for t in range(3)], axis=0).T.astype(BF16)
@@ -255,18 +262,74 @@
         square = c2 * c2
         weighted = c2 * ((square - 2.0) * f0 + f2) + (square - 1.0) * f1
         hall_base[at] = hall_base[at] + hall_gain[at] * weighted
-        return carry
-
-    def accumulate_last(i, carry):
+
+    def accumulate_last(i):
         at = pl.ds(i * deep, deep)
         cols = pl.ds(pl.multiple_of(i * chunk, chunk), chunk)
         e = terms(hall_diff[3, :, cols]).T.astype(BF16)
         forced = mm(e, outer_t[0, :32]).reshape(deep, part_y, nz)
         hall_base[at] = hall_base[at] + hall_gain[at] * forced
-        return carry
 
     pl.semaphore_wait(barrier, groups + slabs - 2)
     hall_put(0)
+
+
+    yz = lax.broadcasted_iota(jnp.int32, (part_y, nz), 0) + column * part_y
+    ky_f = yz.astype(F32)
+    kz_f = iota((part_y, nz), 1)
+    q_yz = (SCALE / ny**2) * (ky_f * ky_f) + (SCALE / nz**2) * (kz_f * kz_f)
+
+    def prepare_first(i):
+        at = pl.ds(i * deep, deep)
+        cols = pl.ds(pl.multiple_of(i * chunk, chunk), chunk)
+        a = (lax.broadcasted_iota(jnp.int32, (deep, part_y, nz), 0) + i * deep).astype(F32)
+        c2, gain = factors((SCALE / nx**2) * (a * a) + q_yz[None])
+        hall_c2[at] = c2
+        hall_gain[at] = gain
+        fresh = c2 * hall_now[at] - hall_prev[at]
+        hall_base[at] = fresh
+        hall_faces[1, :, cols] = spread_of(fresh.reshape(chunk, nz))
+        both = mm_nt(respond_t[0, :96], gain.reshape(chunk, nz).astype(BF16))
+        hall_resp[0, :, cols] = both[:48] + both[48:]
+
+    def prepare_second(i):
+        at = pl.ds(i * deep, deep)
+        cols = pl.ds(pl.multiple_of(i * chunk, chunk), chunk)
+        c2 = hall_c2[at]
+        gain = hall_gain[at]
+        m2 = c2 * hall_base[at] - hall_now[at]
+        hall_faces[2, :, cols] = spread_of(m2.reshape(chunk, nz))
+        s2 = gain * c2
+        s3 = s2 * c2 - gain
+        both = [s.reshape(chunk, nz).astype(BF16) for s in (s2, s3)]
+        both = mm_nt(broad(respond_t), jnp.concatenate(both, axis=1))
+        hall_resp[1, :, cols] = both[:48] + both[48:96]
+        hall_resp[2, :, cols] = both[96:144] + both[144:]
+
+    def prepare_third(i):
+        at = pl.ds(i * deep, deep)
+        cols = pl.ds(pl.multiple_of(i * chunk, chunk), chunk)
+        c2 = hall_c2[at]
+        m1 = hall_base[at]
+        m2 = c2 * m1 - hall_now[at]
+        m3 = c2 * m2 - m1
+        hall_base[at] = c2 * m3 - m2
+        hall_faces[3, :, cols] = spread_of(m3.reshape(chunk, nz))
+
+    copies[1].wait()
+    copies[6].wait()
+    chunks(prepare_first, 2)
+    diff = hall_get(0)
+    hall_respond(0, 1, diff)
+    hall_put(1)
+    chunks(prepare_second, 2)
+    hall_respond(0, 2, diff)
+    diff = hall_get(1)
+    hall_respond(1, 1, diff)
+    hall_put(2)
+    chunks(prepare_third, 2)
+    hall_respond(0, 3, hall_diff[0])
+    hall_respond(1, 2, diff)
 
     lane = lax.broadcasted_iota(jnp.int32, (width, 128), 1)
     kx = lax.broadcasted_iota(jnp.int32, (width, 128), 0)
@@ -415,59 +478,75 @@
             room_put(t + 1)
             room_sent(t)
 
+    diff = hall_get(2)
+    hall_respond(2, 1, diff)
+    hall_put(3)
     room_put(0)
-
-    yz = lax.broadcasted_iota(jnp.int32, (part_y, nz), 0) + column * part_y
-    ky_f = yz.astype(F32)
-    kz_f = iota((part_y, nz), 1)
-    q_yz = (SCALE / ny**2) * (ky_f * ky_f) + (SCALE / nz**2) * (kz_f * kz_f)
-
-    def prepare_first(i, carry):
-        at = pl.ds(i * deep, deep)
-        cols = pl.ds(pl.multiple_of(i * chunk, chunk), chunk)
-        a = (lax.broadcasted_iota(jnp.int32, (deep, part_y, nz), 0) + i * deep).astype(F32)
-        c2, gain = factors((SCALE / nx**2) * (a * a) + q_yz[None])
-        hall_c2[at] = c2
-        hall_gain[at] = gain
-        fresh = c2 * hall_now[at] - hall_prev[at]
-        hall_base[at] = fresh
-        hall_faces[1, :, cols] = spread_of(fresh.reshape(chunk, nz))
-        both = mm_nt(respond_t[0, :96], gain.reshape(chunk, nz).astype(BF16))
-        hall_resp[0, :, cols] = both[:48] + both[48:]
+    copies[7].wait()
+    chunks(accumulate_early, 2)
+    hall_get(3)
+    chunks(accumulate_last, 2)
+
+    parts = 2
+    part_b = part_y // parts
+
+    def a2a_copy(h, step):
+        peer = lax.rem(column + step, slabs)
+        return pltpu.make_async_remote_copy(
+            src_ref=a2a_send.at[pl.ds(part_b * h, part_b), pl.ds(pl.multiple_of(peer * part_x, part_x), part_x), :],
+            dst_ref=a2a_recv.at[pl.ds(column * part_y + part_b * h, part_b)],
+            send_sem=a2a_ssem.at[h, step],
+            recv_sem=a2a_rsem.at[h, step],
+            device_id=(me, peer),
+            device_id_type=MESH,
+        )
+
+    copies[8].wait()
+    for h in range(parts):
+        for b in range(part_b * h, part_b * h + part_b, 2):
+            pair = [stacked(hall_base[:, b + i, :], 0) for i in range(2)]
+            y = mm(broad(cosx_t), jnp.concatenate(pair, axis=1))
+            a2a_send[b] = y[:, :nz]
+            a2a_send[b + 1] = y[:, nz:]
+
+        def a2a_start(i, carry):
+            a2a_copy(h, far_first(i, slabs)).start()
+            return carry
+
+        lax.fori_loop(1, slabs, a2a_start, 0)
+
+    def z_part_of(x):
+        x = stacked(x.reshape(part_y * part_x, nz), 1)
+        return mm(x, cosz_t[...]).reshape(part_y, part_x, nz)
+
+    copies[10].wait()
+    own = pl.ds(pl.multiple_of(column * part_x, part_x), part_x)
+    a2a_recv[pl.ds(column * part_y, part_y)] = z_part_of(a2a_send[:, own, :])
+
+    def a2a_take(i, carry):
+        step = far_first(i, slabs)
+        a2a_copy(0, step).wait_recv()
+        a2a_copy(1, step).wait_recv()
+        source = lax.rem(column + slabs - step, slabs)
+        at = pl.ds(source * part_y, part_y)
+        a2a_recv[at] = z_part_of(a2a_recv[at])
         return carry
 
-    def prepare_last(i, carry):
-        at = pl.ds(i * deep, deep)
-        cols = pl.ds(pl.multiple_of(i * chunk, chunk), chunk)
-        c2 = hall_c2[at]
-        gain = hall_gain[at]
-        m1 = hall_base[at]
-        m2 = c2 * m1 - hall_now[at]
-        m3 = c2 * m2 - m1
-        hall_base[at] = c2 * m3 - m2
-        hall_faces[2, :, cols] = spread_of(m2.reshape(chunk, nz))
-        hall_faces[3, :, cols] = spread_of(m3.reshape(chunk, nz))
-        s2 = gain * c2
-        s3 = s2 * c2 - gain
-        both = [s.reshape(chunk, nz).astype(BF16) for s in (s2, s3)]
-        both = mm_nt(broad(respond_t), jnp.concatenate(both, axis=1))
-        hall_resp[1, :, cols] = both[:48] + both[48:96]
-        hall_resp[2, :, cols] = both[96:144] + both[144:]
+    def room_tables_full(b, carry):
+        for i in range(4):
+            r = 4 * b + i
+            which = jnp.maximum(lengths[0, 0, r] - SHORTEST, 0)
+            at = pl.ds(pl.multiple_of(r * width, width), width)
+            raw_full[at, :] = jnp.where(lane // width == i, room_t[which], 0.0)
         return carry
 
-    copies[1].wait()
-    copies[6].wait()
-    lax.fori_loop(0, lanes // chunk, prepare_first, 0)
-    diff = hall_get(0)
-    hall_respond(0, 1, diff)
-    hall_put(1)
-    lax.fori_loop(0, lanes // chunk, prepare_last, 0)
-    hall_respond(0, 2, diff)
-    hall_respond(0, 3, diff)
-    diff = hall_get(1)
-    hall_respond(1, 1, diff)
-    hall_put(2)
-    hall_respond(1, 2, diff)
+    copies[13].wait()
+    copies[14].wait()
+    lax.fori_loop(0, batches, room_tables_full, 0)
+    for b in range(batches):
+        big = slice(128 * b, 128 * b + 128)
+        high, low = split(raw_full[big, :])
+        full_l[big, :] = jnp.concatenate([high, high, low], axis=1)
 
     q_cross = (lane // SZ).astype(F32) / SY
     q_cross = SCALE * (q_cross * q_cross)
@@ -496,7 +575,6 @@
 
     copies[3].wait()
     copies[12].wait()
-    copies[7].wait()
     lax.fori_loop(0, batches, room_second, 0)
     for b in range(batches):
         x = raw_force[32 * b : 32 * b + 32, :]
@@ -506,75 +584,7 @@
     take_col = jnp.broadcast_to(take_row, (8, wide)).T[:, 0:1]
     take_l[...] = jnp.where(iota((wide, slots), 1) == take_col, 1.0, 0.0).astype(BF16)
 
-    diff = hall_get(2)
-    hall_respond(2, 1, diff)
-    hall_put(3)
     room_step(0)
-    lax.fori_loop(0, lanes // chunk, accumulate_early, 0)
-    hall_get(3)
-    lax.fori_loop(0, lanes // chunk, accumulate_last, 0)
-
-    parts = 2
-    part_b = part_y // parts
-
-    def a2a_copy(h, step):
-        peer = lax.rem(column + step, slabs)
-        return pltpu.make_async_remote_copy(
-            src_ref=a2a_send.at[pl.ds(part_b * h, part_b), pl.ds(pl.multiple_of(peer * part_x, part_x), part_x), :],
-            dst_ref=a2a_recv.at[pl.ds(column * part_y + part_b * h, part_b)],
-            send_sem=a2a_ssem.at[h, step],
-            recv_sem=a2a_rsem.at[h, step],
-            device_id=(me, peer),
-            device_id_type=MESH,
-        )
-
-    copies[8].wait()
-    for h in range(parts):
-        for b in range(part_b * h, part_b * h + part_b, 2):
-            pair = [stacked(hall_base[:, b + i, :], 0) for i in range(2)]
-            y = mm(broad(cosx_t), jnp.concatenate(pair, axis=1))
-            a2a_send[b] = y[:, :nz]
-            a2a_send[b + 1] = y[:, nz:]
-
-        def a2a_start(i, carry):
-            a2a_copy(h, far_first(i, slabs)).start()
-            return carry
-
-        lax.fori_loop(1, slabs, a2a_start, 0)
-
-    def z_part_of(x):
-        x = stacked(x.reshape(part_y * part_x, nz), 1)
-        return mm(x, cosz_t[...]).reshape(part_y, part_x, nz)
-
-    copies[10].wait()
-    own = pl.ds(pl.multiple_of(column * part_x, part_x), part_x)
-    a2a_recv[pl.ds(column * part_y, part_y)] = z_part_of(a2a_send[:, own, :])
-
-    def a2a_take(i, carry):
-        step = far_first(i, slabs)
-        a2a_copy(0, step).wait_recv()
-        a2a_copy(1, step).wait_recv()
-        source = lax.rem(column + slabs - step, slabs)
-        at = pl.ds(source * part_y, part_y)
-        a2a_recv[at] = z_part_of(a2a_recv[at])
-        return carry
-
-    def room_tables_full(b, carry):
-        for i in range(4):
-            r = 4 * b + i
-            which = jnp.maximum(lengths[0, 0, r] - SHORTEST, 0)
-            at = pl.ds(pl.multiple_of(r * width, width), width)
-            raw_full[at, :] = jnp.where(lane // width == i, room_t[which], 0.0)
-        return carry
-
-    copies[13].wait()
-    copies[14].wait()
-    lax.fori_loop(0, batches, room_tables_full, 0)
-    for b in range(batches):
-        big = slice(128 * b, 128 * b + 128)
-        high, low = split(raw_full[big, :])
-        full_l[big, :] = jnp.concatenate([high, high, low], axis=1)
-
     room_step(1)
     for t in range(STEPS - 1):
         hall_copy(t, 0).wait_send()
@@ -607,17 +617,21 @@
         store(1, i).wait()
 
 
-def hand_on(hall_in, room_in, hall_out, room_out, sem):
-    copies = []
-    for j, (near, far) in enumerate(((hall_in, hall_out), (room_in, room_out))):
-        size = near.shape[0] // 8
-        for i in range(8):
+def hand_on(hall_in, room_in, hall_out, room_out, hall_mid, room_mid, load_sem, store_sem):
+    loads, stores = [], []
+    for j, (near, mid, far) in enumerate(((hall_in, hall_mid, hall_out), (room_in, room_mid, room_out))):
+        size = near.shape[0] // 4
+        for i in range(4):
             at = pl.ds(i * size, size)
-            copies.append(pltpu.make_async_copy(near.at[at], far.at[at], sem.at[j, i]))
-    for copy in copies:
-        copy.start()
-    for copy in copies:
-        copy.wait()
+            loads.append(pltpu.make_async_copy(near.at[at], mid.at[at], load_sem.at[j, i]))
+            stores.append(pltpu.make_async_copy(mid.at[at], far.at[at], store_sem.at[j, i]))
+    for load in loads:
+        load.start()
+    for load, store in zip(loads, stores):
+        load.wait()
+        store.start()
+    for store in stores:
+        store.wait()
 
 
 def local(hall_now, hall_prev, room_now, room_prev, room_length, right_neighbor):
@@ -695,7 +709,7 @@
         out_shape=tuple(jax.ShapeDtypeStruct(x.shape, x.dtype) for x in results),
         in_specs=[away] * 2,
         out_specs=(away, away),
-        scratch_shapes=[dma((2, 8))],
+        scratch_shapes=[pltpu.VMEM(x.shape, x.dtype) for x in results] + [dma((2, 4)), dma((2, 4))],
         compiler_params=pltpu.CompilerParams(vmem_limit_bytes=60 * 1024 * 1024),
     )(*results)
     return (hall_pressure[None], room_pressure.reshape(1, 1, count, width, cross))

time: 125 us -> 74.3 us (0.59)
  Pallas kernels: 124 us -> 73 us
    pallas_call x1, Pallas kernels: 48.9 us -> 2.22 us  [local(): pl.pallas_call(hand_on, out_shape=tuple((jax.ShapeDtypeStruct(x.shape, x....]
    pallas_call x1, Pallas kernels: 75 us -> 70.8 us  [local(): pl.pallas_call(functools.partial(kernel, groups, slabs, count, len(inputs...]
where the time goes in v3:
time: 74.3 us; the launch traced here: 73.7 us
  Pallas kernels  73 us (98%)
    pallas_call x1, Pallas kernels, local(): pl.pallas_call(functools.partial(kernel, groups, slabs, count, len(inputs...  70.8 us
    pallas_call x1, Pallas kernels, local(): pl.pallas_call(hand_on, out_shape=tuple((jax.ShapeDtypeStruct(x.shape, x....  2.22 us

profile of v3, /device:TPU:1, one launch (start us, length us, event | category | flops | bytes accessed | tf_op | source)
XLA Modules:
  0.0 73.7 jit_solution(6982226963099996459)
XLA Ops:
  0.6 70.8 %shard_map.167 = (f32[16,128,128]{2,1,0:T(8,128)}, f32[1024,128]{1,0:T(8,128)}) custom-call(s32[1,1,32]{2,1,0:T(1,128)} %refs_0_.1, f32[256,8,128]{2,1,0:T(8,128)} %bitcast.6, f32[256,8,128]{2,1,0:T(8,128)} %bitcast.7, f32[1024,128]{1,0:T(8,128)} %bitcast.8, f32[1024,128]{1,0:T(8,128)} %bitcast.9, s32[1,1024]{1,0:T(1,128)} %refs_5_.1, ...), custom_call_target="tpu_custom_call" | custom-call | tf_op jit(solution)/shard_map/pallas_call | solution.py:656
  71.5 2.2 %shard_map.168 = (f32[16,128,128]{2,1,0:T(8,128)}, f32[1024,128]{1,0:T(8,128)}) custom-call(f32[16,128,128]{2,1,0:T(8,128)} %get-tuple-element.6.hall_in, f32[1024,128]{1,0:T(8,128)} %get-tuple-element.7.room_in), custom_call_target="tpu_custom_call" | custom-call | tf_op jit(solution)/shard_map/pallas_call | solution.py:707

commit v4 on v3

--- a/solution.py
+++ b/solution.py
@@ -146,8 +146,8 @@
         hall_c2, hall_gain, hall_base, hall_faces, hall_resp, hall_diff, hall_other,
         hall_send, hall_recv, a2a_send, a2a_recv,
         room_c2, room_gain, room_a, room_b, room_faces, raw_faces, raw_force, raw_full,
-        face_l, force_l, full_l, pack_l, take_l, room_send, room_recv, hall_out, room_out,
-        load_sem, store_sem, hall_ssem, hall_rsem, a2a_ssem, a2a_rsem, room_ssem, room_rsem,
+        face_l, force_l, full_l, pack_l, take_l, room_send, room_recv, hall_out, room_out, relay,
+        load_sem, store_sem, hall_ssem, hall_rsem, a2a_ssem, a2a_rsem, relay_sem, room_ssem, room_rsem,
     ) = refs
     me = lax.axis_index("grp")
     column = lax.axis_index("slab")
@@ -273,63 +273,6 @@
     pl.semaphore_wait(barrier, groups + slabs - 2)
     hall_put(0)
 
-
-    yz = lax.broadcasted_iota(jnp.int32, (part_y, nz), 0) + column * part_y
-    ky_f = yz.astype(F32)
-    kz_f = iota((part_y, nz), 1)
-    q_yz = (SCALE / ny**2) * (ky_f * ky_f) + (SCALE / nz**2) * (kz_f * kz_f)
-
-    def prepare_first(i):
-        at = pl.ds(i * deep, deep)
-        cols = pl.ds(pl.multiple_of(i * chunk, chunk), chunk)
-        a = (lax.broadcasted_iota(jnp.int32, (deep, part_y, nz), 0) + i * deep).astype(F32)
-        c2, gain = factors((SCALE / nx**2) * (a * a) + q_yz[None])
-        hall_c2[at] = c2
-        hall_gain[at] = gain
-        fresh = c2 * hall_now[at] - hall_prev[at]
-        hall_base[at] = fresh
-        hall_faces[1, :, cols] = spread_of(fresh.reshape(chunk, nz))
-        both = mm_nt(respond_t[0, :96], gain.reshape(chunk, nz).astype(BF16))
-        hall_resp[0, :, cols] = both[:48] + both[48:]
-
-    def prepare_second(i):
-        at = pl.ds(i * deep, deep)
-        cols = pl.ds(pl.multiple_of(i * chunk, chunk), chunk)
-        c2 = hall_c2[at]
-        gain = hall_gain[at]
-        m2 = c2 * hall_base[at] - hall_now[at]
-        hall_faces[2, :, cols] = spread_of(m2.reshape(chunk, nz))
-        s2 = gain * c2
-        s3 = s2 * c2 - gain
-        both = [s.reshape(chunk, nz).astype(BF16) for s in (s2, s3)]
-        both = mm_nt(broad(respond_t), jnp.concatenate(both, axis=1))
-        hall_resp[1, :, cols] = both[:48] + both[48:96]
-        hall_resp[2, :, cols] = both[96:144] + both[144:]
-
-    def prepare_third(i):
-        at = pl.ds(i * deep, deep)
-        cols = pl.ds(pl.multiple_of(i * chunk, chunk), chunk)
-        c2 = hall_c2[at]
-        m1 = hall_base[at]
-        m2 = c2 * m1 - hall_now[at]
-        m3 = c2 * m2 - m1
-        hall_base[at] = c2 * m3 - m2
-        hall_faces[3, :, cols] = spread_of(m3.reshape(chunk, nz))
-
-    copies[1].wait()
-    copies[6].wait()
-    chunks(prepare_first, 2)
-    diff = hall_get(0)
-    hall_respond(0, 1, diff)
-    hall_put(1)
-    chunks(prepare_second, 2)
-    hall_respond(0, 2, diff)
-    diff = hall_get(1)
-    hall_respond(1, 1, diff)
-    hall_put(2)
-    chunks(prepare_third, 2)
-    hall_respond(0, 3, hall_diff[0])
-    hall_respond(1, 2, diff)
 
     lane = lax.broadcasted_iota(jnp.int32, (width, 128), 1)
     kx = lax.broadcasted_iota(jnp.int32, (width, 128), 0)
@@ -410,9 +353,19 @@
         return pltpu.make_async_remote_copy(
             src_ref=room_send.at[t, step],
             dst_ref=room_recv.at[t, step - 1],
-            send_sem=room_ssem.at[t, step - 1],
-            recv_sem=room_rsem.at[t, step - 1],
+            send_sem=room_ssem.at[t],
+            recv_sem=room_rsem.at[t],
             device_id=(lax.rem(me + step, groups), column),
+            device_id_type=MESH,
+        )
+
+    def room_all(t):
+        return pltpu.make_async_remote_copy(
+            src_ref=room_send.at[t, pl.ds(1, groups - 1)],
+            dst_ref=room_recv.at[t],
+            send_sem=room_ssem.at[t],
+            recv_sem=room_rsem.at[t],
+            device_id=(lax.rem(me + 1, groups), column),
             device_id_type=MESH,
         )
 
@@ -441,22 +394,14 @@
         return pltpu.make_async_copy(near.at[at], far.at[at], store_sem.at[which, i])
 
     def room_get(t):
-        def body(i, carry):
-            room_copy(t, far_first(i, groups)).wait_recv()
-            return carry
-
-        lax.fori_loop(1, groups, body, 0)
+        room_all(t).wait_recv()
         got = jnp.concatenate([room_send[t, 0:1], room_recv[t]], axis=0)
         got = jnp.concatenate([got, jnp.zeros((groups, 4, 128), F32)], axis=1).reshape(slots, 128)
         other = mm(take_l[...], two_parts(got))
         return other[:, :128] + other[:, 128:] - room_faces[...]
 
     def room_sent(t):
-        def body(step, carry):
-            room_copy(t, step).wait_send()
-            return carry
-
-        lax.fori_loop(1, groups, body, 0)
+        room_all(t).wait_send()
 
     def room_step(t):
         diff = room_get(t)
@@ -478,10 +423,68 @@
             room_put(t + 1)
             room_sent(t)
 
+    room_put(0)
+
+    yz = lax.broadcasted_iota(jnp.int32, (part_y, nz), 0) + column * part_y
+    ky_f = yz.astype(F32)
+    kz_f = iota((part_y, nz), 1)
+    q_yz = (SCALE / ny**2) * (ky_f * ky_f) + (SCALE / nz**2) * (kz_f * kz_f)
+
+    def prepare_first(i):
+        at = pl.ds(i * deep, deep)
+        cols = pl.ds(pl.multiple_of(i * chunk, chunk), chunk)
+        a = (lax.broadcasted_iota(jnp.int32, (deep, part_y, nz), 0) + i * deep).astype(F32)
+        c2, gain = factors((SCALE / nx**2) * (a * a) + q_yz[None])
+        hall_c2[at] = c2
+        hall_gain[at] = gain
+        fresh = c2 * hall_now[at] - hall_prev[at]
+        hall_base[at] = fresh
+        hall_faces[1, :, cols] = spread_of(fresh.reshape(chunk, nz))
+        both = mm_nt(respond_t[0, :96], gain.reshape(chunk, nz).astype(BF16))
+        hall_resp[0, :, cols] = both[:48] + both[48:]
+
+    def prepare_second(i):
+        at = pl.ds(i * deep, deep)
+        cols = pl.ds(pl.multiple_of(i * chunk, chunk), chunk)
+        c2 = hall_c2[at]
+        gain = hall_gain[at]
+        m2 = c2 * hall_base[at] - hall_now[at]
+        hall_faces[2, :, cols] = spread_of(m2.reshape(chunk, nz))
+        s2 = gain * c2
+        s3 = s2 * c2 - gain
+        both = [s.reshape(chunk, nz).astype(BF16) for s in (s2, s3)]
+        both = mm_nt(broad(respond_t), jnp.concatenate(both, axis=1))
+        hall_resp[1, :, cols] = both[:48] + both[48:96]
+        hall_resp[2, :, cols] = both[96:144] + both[144:]
+
+    def prepare_third(i):
+        at = pl.ds(i * deep, deep)
+        cols = pl.ds(pl.multiple_of(i * chunk, chunk), chunk)
+        c2 = hall_c2[at]
+        m1 = hall_base[at]
+        m2 = c2 * m1 - hall_now[at]
+        m3 = c2 * m2 - m1
+        hall_base[at] = c2 * m3 - m2
+        hall_faces[3, :, cols] = spread_of(m3.reshape(chunk, nz))
+
+    copies[1].wait()
+    copies[6].wait()
+    chunks(prepare_first, 2)
+    diff = hall_get(0)
+    hall_respond(0, 1, diff)
+    hall_put(1)
+    chunks(prepare_second, 2)
+    hall_respond(0, 2, diff)
+    diff = hall_get(1)
+    hall_respond(1, 1, diff)
+    hall_put(2)
+    chunks(prepare_third, 2)
+    hall_respond(0, 3, hall_diff[0])
+    hall_respond(1, 2, diff)
+
     diff = hall_get(2)
     hall_respond(2, 1, diff)
     hall_put(3)
-    room_put(0)
     copies[7].wait()
     chunks(accumulate_early, 2)
     hall_get(3)
@@ -490,16 +493,49 @@
     parts = 2
     part_b = part_y // parts
 
-    def a2a_copy(h, step):
-        peer = lax.rem(column + step, slabs)
+    ring = slabs // 2
+    chip = column // 2
+    core = lax.rem(column, 2)
+    relayed = ring == 8
+
+    def column_of(hops, k):
+        return 2 * lax.rem(chip + hops + ring, ring) + k
+
+    def a2a_copy(h, hops, k, source_core):
+        peer = column_of(hops, k)
         return pltpu.make_async_remote_copy(
             src_ref=a2a_send.at[pl.ds(part_b * h, part_b), pl.ds(pl.multiple_of(peer * part_x, part_x), part_x), :],
             dst_ref=a2a_recv.at[pl.ds(column * part_y + part_b * h, part_b)],
-            send_sem=a2a_ssem.at[h, step],
-            recv_sem=a2a_rsem.at[h, step],
+            send_sem=a2a_ssem.at[h, 2 * hops + k],
+            recv_sem=a2a_rsem.at[h, 2 * hops + source_core],
             device_id=(me, peer),
             device_id_type=MESH,
         )
+
+    def relay_copy(h):
+        far = pl.multiple_of(column_of(ring // 2, 0) * part_x, 2 * part_x)
+        return pltpu.make_async_remote_copy(
+            src_ref=a2a_send.at[pl.ds(part_b * h, part_b), pl.ds(far, 2 * part_x), :],
+            dst_ref=relay.at[h],
+            send_sem=relay_sem.at[h, 0],
+            recv_sem=relay_sem.at[h, 1],
+            device_id=(me, column_of(1 - 2 * h, core)),
+            device_id_type=MESH,
+        )
+
+    def forward_copy(h, k):
+        way = 1 - 2 * h
+        source = column_of(-way, core)
+        return pltpu.make_async_remote_copy(
+            src_ref=relay.at[h, :, pl.ds(k * part_x, part_x), :],
+            dst_ref=a2a_recv.at[pl.ds(source * part_y + part_b * h, part_b)],
+            send_sem=relay_sem.at[h, 2 + k],
+            recv_sem=a2a_rsem.at[h, ring + core],
+            device_id=(me, column_of(3 * way, k)),
+            device_id_type=MESH,
+        )
+
+    first_hop = 2 if relayed else 1
 
     copies[8].wait()
     for h in range(parts):
@@ -509,11 +545,15 @@
             a2a_send[b] = y[:, :nz]
             a2a_send[b + 1] = y[:, nz:]
 
+        if relayed:
+            relay_copy(h).start()
+
         def a2a_start(i, carry):
-            a2a_copy(h, far_first(i, slabs)).start()
+            a2a_copy(h, far_first(i // 2, ring), lax.rem(i, 2), core).start()
             return carry
 
-        lax.fori_loop(1, slabs, a2a_start, 0)
+        lax.fori_loop(2 * first_hop, 2 * ring, a2a_start, 0)
+        a2a_copy(h, 0, 1 - core, core).start()
 
     def z_part_of(x):
         x = stacked(x.reshape(part_y * part_x, nz), 1)
@@ -523,13 +563,15 @@
     own = pl.ds(pl.multiple_of(column * part_x, part_x), part_x)
     a2a_recv[pl.ds(column * part_y, part_y)] = z_part_of(a2a_send[:, own, :])
 
+    def take_from(hops, k):
+        a2a_copy(0, hops, k, k).wait_recv()
+        a2a_copy(1, hops, k, k).wait_recv()
+        at = pl.ds(column_of(-hops, k) * part_y, part_y)
+        a2a_recv[at] = z_part_of(a2a_recv[at])
+
     def a2a_take(i, carry):
-        step = far_first(i, slabs)
-        a2a_copy(0, step).wait_recv()
-        a2a_copy(1, step).wait_recv()
-        source = lax.rem(column + slabs - step, slabs)
-        at = pl.ds(source * part_y, part_y)
-        a2a_recv[at] = z_part_of(a2a_recv[at])
+        i = 2 * ring + 2 * first_hop - 1 - i
+        take_from(far_first(i // 2, ring), lax.rem(i, 2))
         return carry
 
     def room_tables_full(b, carry):
@@ -584,6 +626,11 @@
     take_col = jnp.broadcast_to(take_row, (8, wide)).T[:, 0:1]
     take_l[...] = jnp.where(iota((wide, slots), 1) == take_col, 1.0, 0.0).astype(BF16)
 
+    if relayed:
+        for h in range(parts):
+            relay_copy(h).wait_recv()
+            forward_copy(h, 0).start()
+            forward_copy(h, 1).start()
     room_step(0)
     room_step(1)
     for t in range(STEPS - 1):
@@ -592,7 +639,11 @@
     room_step(2)
     hall_copy(3, 0).wait_send()
     hall_copy(3, 1).wait_send()
-    lax.fori_loop(1, slabs, a2a_take, 0)
+    take_from(0, 1 - core)
+    lax.fori_loop(2 * first_hop, 2 * ring, a2a_take, 0)
+    if relayed:
+        take_from(ring // 2, 0)
+        take_from(ring // 2, 1)
     copies[9].wait()
     for x in range(0, part_x, 2):
         pair = jnp.concatenate([stacked(a2a_recv[:, x, :], 0), stacked(a2a_recv[:, x + 1, :], 0)], axis=1)
@@ -605,12 +656,19 @@
     room_step(3)
     room_sent(3)
 
-    def a2a_sent(step, carry):
-        a2a_copy(0, step).wait_send()
-        a2a_copy(1, step).wait_send()
-        return carry
-
-    lax.fori_loop(1, slabs, a2a_sent, 0)
+    for h in range(parts):
+
+        def a2a_sent(i, carry):
+            a2a_copy(h, far_first(i // 2, ring), lax.rem(i, 2), core).wait_send()
+            return carry
+
+        lax.fori_loop(2 * first_hop, 2 * ring, a2a_sent, 0)
+        a2a_copy(h, 0, 1 - core, core).wait_send()
+        if relayed:
+            relay_copy(h).wait_send()
+            forward_copy(h, 0).wait_send()
+            forward_copy(h, 1).wait_send()
+
     for i in range(8):
         store(0, i).wait()
     for i in range(batches):
@@ -691,14 +749,16 @@
             pltpu.VMEM((STEPS, groups - 1, 12, 128), F32),
             pltpu.VMEM((part_x, ny, nz), F32),
             pltpu.VMEM((rows, cross), F32),
+            pltpu.VMEM((2, part_y // 2, 2 * part_x, nz), F32),
             dma((len(inputs),)),
             dma((2, 8)),
             dma((STEPS, 2)),
             dma((STEPS, 2)),
             dma((2, slabs)),
             dma((2, slabs)),
-            dma((STEPS, groups - 1)),
-            dma((STEPS, groups - 1)),
+            dma((2, 4)),
+            dma((STEPS,)),
+            dma((STEPS,)),
         ],
         compiler_params=pltpu.CompilerParams(
             collective_id=0, has_side_effects=True, vmem_limit_bytes=60 * 1024 * 1024

time: 74.3 us -> 83.3 us (1.12)
  the two profiles are of different devices: /device:TPU:1 before, /device:TPU:8 now
where the time goes in v4:
time: 83.3 us; the launch traced here: 83.1 us
  Pallas kernels  82.3 us (99%)
    pallas_call x1, Pallas kernels, local(): pl.pallas_call(functools.partial(kernel, groups, slabs, count, len(inputs...  80.1 us
    pallas_call x1, Pallas kernels, local(): pl.pallas_call(hand_on, out_shape=tuple((jax.ShapeDtypeStruct(x.shape, x....  2.22 us

profile of v4, /device:TPU:8, one launch (start us, length us, event | category | flops | bytes accessed | tf_op | source)
XLA Modules:
  0.0 83.1 jit_solution(14749939228531893684)
XLA Ops:
  0.6 80.1 %shard_map.167 = (f32[16,128,128]{2,1,0:T(8,128)}, f32[1024,128]{1,0:T(8,128)}) custom-call(s32[1,1,32]{2,1,0:T(1,128)} %refs_0_.1, f32[256,8,128]{2,1,0:T(8,128)} %bitcast.6, f32[256,8,128]{2,1,0:T(8,128)} %bitcast.7, f32[1024,128]{1,0:T(8,128)} %bitcast.8, f32[1024,128]{1,0:T(8,128)} %bitcast.9, s32[1,1024]{1,0:T(1,128)} %refs_5_.1, ...), custom_call_target="tpu_custom_call" | custom-call | tf_op jit(solution)/shard_map/pallas_call | solution.py:714
  80.8 2.2 %shard_map.168 = (f32[16,128,128]{2,1,0:T(8,128)}, f32[1024,128]{1,0:T(8,128)}) custom-call(f32[16,128,128]{2,1,0:T(8,128)} %get-tuple-element.6.hall_in, f32[1024,128]{1,0:T(8,128)} %get-tuple-element.7.room_in), custom_call_target="tpu_custom_call" | custom-call | tf_op jit(solution)/shard_map/pallas_call | solution.py:767

commit v5 on v4

--- a/solution.py
+++ b/solution.py
@@ -275,6 +275,9 @@
 
 
     lane = lax.broadcasted_iota(jnp.int32, (width, 128), 1)
+    shift = int(math.log2(width))
+    blocks = [(lane >> shift) == i for i in range(4)]
+    blocks8 = [block[:8] for block in blocks]
     kx = lax.broadcasted_iota(jnp.int32, (width, 128), 0)
 
     def room_first(b, carry):
@@ -284,8 +287,7 @@
             which = jnp.maximum(length - SHORTEST, 0)
             at = pl.ds(pl.multiple_of(r * width, width), width)
             at8 = pl.ds(pl.multiple_of(r * 8, 8), 8)
-            mine = lane // width == i
-            raw_faces[at8, :] = jnp.where(mine[:8], face_t[which], 0.0)
+            raw_faces[at8, :] = jnp.where(blocks8[i], face_t[which], 0.0)
             room_a[at, :] = jnp.where(kx < jnp.full((width, 128), length, jnp.int32), room_now[at, :], 0.0)
         return carry
 
@@ -482,9 +484,47 @@
     hall_respond(0, 3, hall_diff[0])
     hall_respond(1, 2, diff)
 
+    q_cross = (lane >> int(math.log2(SZ))).astype(F32) * (1.0 / SY)
+    q_cross = SCALE * (q_cross * q_cross)
+    z_part = (lane & (SZ - 1)).astype(F32) * (1.0 / SZ)
+    q_cross = q_cross + SCALE * (z_part * z_part)
+    kx_f = kx.astype(F32)
+    kx_sq = SCALE * (kx_f * kx_f)
+
+    def room_second(b, carry):
+        for i in range(4):
+            r = 4 * b + i
+            length = lengths[0, 0, r]
+            which = jnp.maximum(length - SHORTEST, 0)
+            at = pl.ds(pl.multiple_of(r * width, width), width)
+            at8 = pl.ds(pl.multiple_of(r * 8, 8), 8)
+            raw_force[at8, :] = jnp.where(blocks8[i], force_t[which], 0.0)
+            extent = jnp.full((width, 128), length, jnp.int32)
+            live = kx < extent
+            extent = extent[:8].astype(F32)
+            inverse = 1.0 / (extent * extent)
+            inverse = jnp.concatenate([inverse] * (width // 8), axis=0)
+            c2, gain = factors(kx_sq * inverse + q_cross)
+            room_c2[at, :] = c2
+            room_gain[at, :] = gain
+            room_b[at, :] = jnp.where(live, room_prev[at, :], 0.0)
+        return carry
+
+    copies[3].wait()
+    copies[12].wait()
+    lax.fori_loop(0, batches, room_second, 0)
+    for b in range(batches):
+        x = raw_force[32 * b : 32 * b + 32, :]
+        high = x.astype(BF16).astype(F32)
+        low = x - high
+        force_l[128 * b : 128 * b + 128, :] = jnp.concatenate([high, high, low, low], axis=0).T.astype(BF16)
+    take_col = jnp.broadcast_to(take_row, (8, wide)).T[:, 0:1]
+    take_l[...] = jnp.where(iota((wide, slots), 1) == take_col, 1.0, 0.0).astype(BF16)
+
     diff = hall_get(2)
     hall_respond(2, 1, diff)
     hall_put(3)
+    room_step(0)
     copies[7].wait()
     chunks(accumulate_early, 2)
     hall_get(3)
@@ -579,7 +619,7 @@
             r = 4 * b + i
             which = jnp.maximum(lengths[0, 0, r] - SHORTEST, 0)
             at = pl.ds(pl.multiple_of(r * width, width), width)
-            raw_full[at, :] = jnp.where(lane // width == i, room_t[which], 0.0)
+            raw_full[at, :] = jnp.where(blocks[i], room_t[which], 0.0)
         return carry
 
     copies[13].wait()
@@ -590,49 +630,12 @@
         high, low = split(raw_full[big, :])
         full_l[big, :] = jnp.concatenate([high, high, low], axis=1)
 
-    q_cross = (lane // SZ).astype(F32) / SY
-    q_cross = SCALE * (q_cross * q_cross)
-    z_part = (lane % SZ).astype(F32) / SZ
-    q_cross = q_cross + SCALE * (z_part * z_part)
-    kx_f = kx.astype(F32)
-    kx_sq = SCALE * (kx_f * kx_f)
-
-    def room_second(b, carry):
-        for i in range(4):
-            r = 4 * b + i
-            length = lengths[0, 0, r]
-            which = jnp.maximum(length - SHORTEST, 0)
-            at = pl.ds(pl.multiple_of(r * width, width), width)
-            at8 = pl.ds(pl.multiple_of(r * 8, 8), 8)
-            mine = lane // width == i
-            raw_force[at8, :] = jnp.where(mine[:8], force_t[which], 0.0)
-            extent = jnp.full((width, 128), length, jnp.int32)
-            live = kx < extent
-            extent = extent.astype(F32)
-            c2, gain = factors(kx_sq / (extent * extent) + q_cross)
-            room_c2[at, :] = c2
-            room_gain[at, :] = gain
-            room_b[at, :] = jnp.where(live, room_prev[at, :], 0.0)
-        return carry
-
-    copies[3].wait()
-    copies[12].wait()
-    lax.fori_loop(0, batches, room_second, 0)
-    for b in range(batches):
-        x = raw_force[32 * b : 32 * b + 32, :]
-        high = x.astype(BF16).astype(F32)
-        low = x - high
-        force_l[128 * b : 128 * b + 128, :] = jnp.concatenate([high, high, low, low], axis=0).T.astype(BF16)
-    take_col = jnp.broadcast_to(take_row, (8, wide)).T[:, 0:1]
-    take_l[...] = jnp.where(iota((wide, slots), 1) == take_col, 1.0, 0.0).astype(BF16)
-
+    room_step(1)
     if relayed:
         for h in range(parts):
             relay_copy(h).wait_recv()
             forward_copy(h, 0).start()
             forward_copy(h, 1).start()
-    room_step(0)
-    room_step(1)
     for t in range(STEPS - 1):
         hall_copy(t, 0).wait_send()
         hall_copy(t, 1).wait_send()

time: 83.3 us -> 73.1 us (0.88)
  the two profiles are of different devices: /device:TPU:8 before, /device:TPU:1 now
where the time goes in v5:
time: 73.1 us; the launch traced here: 73 us
  Pallas kernels  72.2 us (99%)
  between operations  0.8 us (1%)
    pallas_call x1, Pallas kernels, local(): pl.pallas_call(functools.partial(kernel, groups, slabs, count, len(inputs...  70 us
    pallas_call x1, Pallas kernels, local(): pl.pallas_call(hand_on, out_shape=tuple((jax.ShapeDtypeStruct(x.shape, x....  2.22 us

profile of v5, /device:TPU:1, one launch (start us, length us, event | category | flops | bytes accessed | tf_op | source)
XLA Modules:
  0.0 73.0 jit_solution(4821265985277428020)
XLA Ops:
  0.6 70.0 %shard_map.167 = (f32[16,128,128]{2,1,0:T(8,128)}, f32[1024,128]{1,0:T(8,128)}) custom-call(s32[1,1,32]{2,1,0:T(1,128)} %refs_0_.1, f32[256,8,128]{2,1,0:T(8,128)} %bitcast.6, f32[256,8,128]{2,1,0:T(8,128)} %bitcast.7, f32[1024,128]{1,0:T(8,128)} %bitcast.8, f32[1024,128]{1,0:T(8,128)} %bitcast.9, s32[1,1024]{1,0:T(1,128)} %refs_5_.1, ...), custom_call_target="tpu_custom_call" | custom-call | tf_op jit(solution)/shard_map/pallas_call | solution.py:717
  70.6 2.2 %shard_map.168 = (f32[16,128,128]{2,1,0:T(8,128)}, f32[1024,128]{1,0:T(8,128)}) custom-call(f32[16,128,128]{2,1,0:T(8,128)} %get-tuple-element.6.hall_in, f32[1024,128]{1,0:T(8,128)} %get-tuple-element.7.room_in), custom_call_target="tpu_custom_call" | custom-call | tf_op jit(solution)/shard_map/pallas_call | solution.py:770

commit v6 on v5

--- a/solution.py
+++ b/solution.py
@@ -526,9 +526,9 @@
     hall_put(3)
     room_step(0)
     copies[7].wait()
-    chunks(accumulate_early, 2)
+    chunks(accumulate_early, 4)
     hall_get(3)
-    chunks(accumulate_last, 2)
+    chunks(accumulate_last, 4)
 
     parts = 2
     part_b = part_y // parts
@@ -596,23 +596,32 @@
         a2a_copy(h, 0, 1 - core, core).start()
 
     def z_part_of(x):
-        x = stacked(x.reshape(part_y * part_x, nz), 1)
-        return mm(x, cosz_t[...]).reshape(part_y, part_x, nz)
+        rows = stacked(x.reshape(x.shape[0] * part_x, nz), 1)
+        return mm(rows, cosz_t[...]).reshape(x.shape)
 
     copies[10].wait()
     own = pl.ds(pl.multiple_of(column * part_x, part_x), part_x)
     a2a_recv[pl.ds(column * part_y, part_y)] = z_part_of(a2a_send[:, own, :])
 
-    def take_from(hops, k):
-        a2a_copy(0, hops, k, k).wait_recv()
-        a2a_copy(1, hops, k, k).wait_recv()
-        at = pl.ds(column_of(-hops, k) * part_y, part_y)
-        a2a_recv[at] = z_part_of(a2a_recv[at])
-
-    def a2a_take(i, carry):
-        i = 2 * ring + 2 * first_hop - 1 - i
-        take_from(far_first(i // 2, ring), lax.rem(i, 2))
-        return carry
+    def take_from(h, hops, kinds):
+        spots = []
+        for k in kinds:
+            a2a_copy(h, hops, k, k).wait_recv()
+            spots.append(pl.ds(column_of(-hops, k) * part_y + part_b * h, part_b))
+        x = jnp.concatenate([a2a_recv[at] for at in spots], axis=0)
+        x = z_part_of(x)
+        for i, at in enumerate(spots):
+            a2a_recv[at] = x[part_b * i : part_b * (i + 1)]
+
+    def take_half(h):
+        def body(i, carry):
+            take_from(h, far_first(i, ring), (0, 1))
+            return carry
+
+        lax.fori_loop(first_hop, ring, body, 0)
+        take_from(h, 0, (1 - core,))
+        if relayed:
+            take_from(h, ring // 2, (0, 1))
 
     def room_tables_full(b, carry):
         for i in range(4):
@@ -642,11 +651,8 @@
     room_step(2)
     hall_copy(3, 0).wait_send()
     hall_copy(3, 1).wait_send()
-    take_from(0, 1 - core)
-    lax.fori_loop(2 * first_hop, 2 * ring, a2a_take, 0)
-    if relayed:
-        take_from(ring // 2, 0)
-        take_from(ring // 2, 1)
+    take_half(0)
+    take_half(1)
     copies[9].wait()
     for x in range(0, part_x, 2):
         pair = jnp.concatenate([stacked(a2a_recv[:, x, :], 0), stacked(a2a_recv[:, x + 1, :], 0)], axis=1)
@@ -681,8 +687,8 @@
 def hand_on(hall_in, room_in, hall_out, room_out, hall_mid, room_mid, load_sem, store_sem):
     loads, stores = [], []
     for j, (near, mid, far) in enumerate(((hall_in, hall_mid, hall_out), (room_in, room_mid, room_out))):
-        size = near.shape[0] // 4
-        for i in range(4):
+        size = near.shape[0] // 8
+        for i in range(8):
             at = pl.ds(i * size, size)
             loads.append(pltpu.make_async_copy(near.at[at], mid.at[at], load_sem.at[j, i]))
             stores.append(pltpu.make_async_copy(mid.at[at], far.at[at], store_sem.at[j, i]))
@@ -772,7 +778,7 @@
         out_shape=tuple(jax.ShapeDtypeStruct(x.shape, x.dtype) for x in results),
         in_specs=[away] * 2,
         out_specs=(away, away),
-        scratch_shapes=[pltpu.VMEM(x.shape, x.dtype) for x in results] + [dma((2, 4)), dma((2, 4))],
+        scratch_shapes=[pltpu.VMEM(x.shape, x.dtype) for x in results] + [dma((2, 8)), dma((2, 8))],
         compiler_params=pltpu.CompilerParams(vmem_limit_bytes=60 * 1024 * 1024),
     )(*results)
     return (hall_pressure[None], room_pressure.reshape(1, 1, count, width, cross))

time: 73.1 us -> 73.8 us (level)
  no operation moved by 1% of the time
where the time goes in v6:
time: 73.8 us; the launch traced here: 73.6 us
  Pallas kernels  72.8 us (99%)
  between operations  0.8 us (1%)
    pallas_call x1, Pallas kernels, local(): pl.pallas_call(functools.partial(kernel, groups, slabs, count, len(inputs...  70.4 us
    pallas_call x1, Pallas kernels, local(): pl.pallas_call(hand_on, out_shape=tuple((jax.ShapeDtypeStruct(x.shape, x....  2.39 us

profile of v6, /device:TPU:1, one launch (start us, length us, event | category | flops | bytes accessed | tf_op | source)
XLA Modules:
  0.0 73.6 jit_solution(18280069085501958999)
XLA Ops:
  0.6 70.4 %shard_map.167 = (f32[16,128,128]{2,1,0:T(8,128)}, f32[1024,128]{1,0:T(8,128)}) custom-call(s32[1,1,32]{2,1,0:T(1,128)} %refs_0_.1, f32[256,8,128]{2,1,0:T(8,128)} %bitcast.6, f32[256,8,128]{2,1,0:T(8,128)} %bitcast.7, f32[1024,128]{1,0:T(8,128)} %bitcast.8, f32[1024,128]{1,0:T(8,128)} %bitcast.9, s32[1,1024]{1,0:T(1,128)} %refs_5_.1, ...), custom_call_target="tpu_custom_call" | custom-call | tf_op jit(solution)/shard_map/pallas_call | solution.py:723
  71.1 2.4 %shard_map.168 = (f32[16,128,128]{2,1,0:T(8,128)}, f32[1024,128]{1,0:T(8,128)}) custom-call(f32[16,128,128]{2,1,0:T(8,128)} %get-tuple-element.6.hall_in, f32[1024,128]{1,0:T(8,128)} %get-tuple-element.7.room_in), custom_call_target="tpu_custom_call" | custom-call | tf_op jit(solution)/shard_map/pallas_call | solution.py:776

commit v7 on v6

--- a/solution.py
+++ b/solution.py
@@ -252,23 +252,16 @@
         low = e - high
         return jnp.concatenate([high, low, high, low], axis=0)
 
-    def accumulate_early(i):
+    def accumulate(i):
         at = pl.ds(i * deep, deep)
         cols = pl.ds(pl.multiple_of(i * chunk, chunk), chunk)
-        e = jnp.concatenate([terms(hall_diff[t, :, cols]) for t in range(3)], axis=0).T.astype(BF16)
-        forced = mm(e, broad(outer_t, 3, 96))
+        e = jnp.concatenate([terms(hall_diff[t, :, cols]) for t in range(STEPS)], axis=0).T.astype(BF16)
+        forced = mm(e, broad(outer_t))
         c2 = hall_c2[at]
-        f0, f1, f2 = [forced[:, 128 * t : 128 * t + 128].reshape(deep, part_y, nz) for t in range(3)]
+        f0, f1, f2, f3 = [forced[:, 128 * t : 128 * t + 128].reshape(deep, part_y, nz) for t in range(STEPS)]
         square = c2 * c2
-        weighted = c2 * ((square - 2.0) * f0 + f2) + (square - 1.0) * f1
+        weighted = c2 * ((square - 2.0) * f0 + f2) + (square - 1.0) * f1 + f3
         hall_base[at] = hall_base[at] + hall_gain[at] * weighted
-
-    def accumulate_last(i):
-        at = pl.ds(i * deep, deep)
-        cols = pl.ds(pl.multiple_of(i * chunk, chunk), chunk)
-        e = terms(hall_diff[3, :, cols]).T.astype(BF16)
-        forced = mm(e, outer_t[0, :32]).reshape(deep, part_y, nz)
-        hall_base[at] = hall_base[at] + hall_gain[at] * forced
 
     pl.semaphore_wait(barrier, groups + slabs - 2)
     hall_put(0)
@@ -383,11 +376,14 @@
         packed = packed[:, :128] + packed[:, 128:]
         room_send[t] = packed.reshape(groups, 16, 128)[:, :12, :]
 
+        room_copy(t, groups // 2).start()
+
         def body(i, carry):
-            room_copy(t, far_first(i, groups)).start()
+            room_copy(t, groups // 2 + i).start()
+            room_copy(t, groups // 2 - i).start()
             return carry
 
-        lax.fori_loop(1, groups, body, 0)
+        lax.fori_loop(1, groups // 2, body, 0)
 
     def store(which, i):
         near, far = ((hall_out, hall_far), (room_out, room_far))[which]
@@ -526,9 +522,8 @@
     hall_put(3)
     room_step(0)
     copies[7].wait()
-    chunks(accumulate_early, 4)
     hall_get(3)
-    chunks(accumulate_last, 4)
+    chunks(accumulate, 4)
 
     parts = 2
     part_b = part_y // parts
@@ -589,10 +584,11 @@
             relay_copy(h).start()
 
         def a2a_start(i, carry):
-            a2a_copy(h, far_first(i // 2, ring), lax.rem(i, 2), core).start()
+            a2a_copy(h, far_first(i, ring), 0, core).start()
+            a2a_copy(h, far_first(i, ring), 1, core).start()
             return carry
 
-        lax.fori_loop(2 * first_hop, 2 * ring, a2a_start, 0)
+        lax.fori_loop(first_hop, ring, a2a_start, 0)
         a2a_copy(h, 0, 1 - core, core).start()
 
     def z_part_of(x):
@@ -687,8 +683,8 @@
 def hand_on(hall_in, room_in, hall_out, room_out, hall_mid, room_mid, load_sem, store_sem):
     loads, stores = [], []
     for j, (near, mid, far) in enumerate(((hall_in, hall_mid, hall_out), (room_in, room_mid, room_out))):
-        size = near.shape[0] // 8
-        for i in range(8):
+        size = near.shape[0] // 4
+        for i in range(4):
             at = pl.ds(i * size, size)
             loads.append(pltpu.make_async_copy(near.at[at], mid.at[at], load_sem.at[j, i]))
             stores.append(pltpu.make_async_copy(mid.at[at], far.at[at], store_sem.at[j, i]))
@@ -778,7 +774,7 @@
         out_shape=tuple(jax.ShapeDtypeStruct(x.shape, x.dtype) for x in results),
         in_specs=[away] * 2,
         out_specs=(away, away),
-        scratch_shapes=[pltpu.VMEM(x.shape, x.dtype) for x in results] + [dma((2, 8)), dma((2, 8))],
+        scratch_shapes=[pltpu.VMEM(x.shape, x.dtype) for x in results] + [dma((2, 4)), dma((2, 4))],
         compiler_params=pltpu.CompilerParams(vmem_limit_bytes=60 * 1024 * 1024),
     )(*results)
     return (hall_pressure[None], room_pressure.reshape(1, 1, count, width, cross))

time: 73.8 us -> 72.2 us (0.978)
  Pallas kernels: 72.8 us -> 71.3 us
    pallas_call x1, Pallas kernels: 70.4 us -> 69 us  [local(): pl.pallas_call(functools.partial(kernel, groups, slabs, count, len(inputs...]
where the time goes in v7:
time: 72.2 us; the launch traced here: 72.1 us
  Pallas kernels  71.3 us (99%)
  between operations  0.8 us (1%)
    pallas_call x1, Pallas kernels, local(): pl.pallas_call(functools.partial(kernel, groups, slabs, count, len(inputs...  69 us
    pallas_call x1, Pallas kernels, local(): pl.pallas_call(hand_on, out_shape=tuple((jax.ShapeDtypeStruct(x.shape, x....  2.22 us

profile of v7, /device:TPU:1, one launch (start us, length us, event | category | flops | bytes accessed | tf_op | source)
XLA Modules:
  0.0 72.1 jit_solution(3147475962029930006)
XLA Ops:
  0.6 69.0 %shard_map.167 = (f32[16,128,128]{2,1,0:T(8,128)}, f32[1024,128]{1,0:T(8,128)}) custom-call(s32[1,1,32]{2,1,0:T(1,128)} %refs_0_.1, f32[256,8,128]{2,1,0:T(8,128)} %bitcast.6, f32[256,8,128]{2,1,0:T(8,128)} %bitcast.7, f32[1024,128]{1,0:T(8,128)} %bitcast.8, f32[1024,128]{1,0:T(8,128)} %bitcast.9, s32[1,1024]{1,0:T(1,128)} %refs_5_.1, ...), custom_call_target="tpu_custom_call" | custom-call | tf_op jit(solution)/shard_map/pallas_call | solution.py:719
  69.7 2.2 %shard_map.168 = (f32[16,128,128]{2,1,0:T(8,128)}, f32[1024,128]{1,0:T(8,128)}) custom-call(f32[16,128,128]{2,1,0:T(8,128)} %get-tuple-element.6.hall_in, f32[1024,128]{1,0:T(8,128)} %get-tuple-element.7.room_in), custom_call_target="tpu_custom_call" | custom-call | tf_op jit(solution)/shard_map/pallas_call | solution.py:772
